TPU v7x, 32 devices: a whole 2x2x4 slice. The times are simulated.
32 devices in a mesh: dp: 8 (over z, x), tensor: 4 (over y, core).
Axes of the slice: x: 2, y: 2, z: 4, core: 2. Of those that a mesh axis runs over, the one named last changes fastest.
Arguments:
- block_input: bfloat16 [8192, 1152], P('dp'), may hold values from -24 to 24
- conditions: float32 [32, 1152], replicated, may hold values from -6 to 6
- segment_ids: int32 [8, 1024], P('dp'), may hold values from 0 to 7, never falling along the last dimension, each value on 1 to 256 neighbouring positions
- segment_cond: int32 [8, 8], P('dp'), may hold values from 0 to 31
- cotangent: bfloat16 [8192, 1152], P('dp'), may hold values from -6 to 6
- qkv_weight: float32 [1152, 3, 1152], P('dp', None, 'tensor'), may hold values from -0.1875 to 0.1875
- proj_weight: float32 [1152, 1152], P(('tensor', 'dp')), may hold values from -1.5 to 1.5
- inner_weight: float32 [1152, 4608], P('dp', 'tensor'), may hold values from -0.1875 to 0.1875
- outer_weight: float32 [4608, 1152], P(('tensor', 'dp')), may hold values from -0.1875 to 0.1875
- ada_weight: float32 [6, 1152, 1152], P(None, 'tensor'), may hold values from -0.1875 to 0.1875
- head_biases: float32 [9, 1152], P(None, 'tensor'), may hold values from -1.8 to 1.8
- inner_bias: float32 [4608], P('tensor'), may hold values from -1.8 to 1.8
- shared_biases: float32 [2, 1152], replicated, may hold values from -1.8 to 1.8
- qkv_first: float32 [1152, 3, 1152], P('dp', None, 'tensor'), may hold values from -160 to 160
- proj_first: float32 [1152, 1152], P(('tensor', 'dp')), may hold values from -32 to 32
- inner_first: float32 [1152, 4608], P('dp', 'tensor'), may hold values from -256 to 256
- outer_first: float32 [4608, 1152], P(('tensor', 'dp')), may hold values from -192 to 192
- ada_first: float32 [6, 1152, 1152], P(None, 'tensor'), may hold values from -320 to 320
- head_biases_first: float32 [9, 1152], P(None, 'tensor'), may hold values from -384 to 384
- inner_bias_first: float32 [4608], P('tensor'), may hold values from -256 to 256
- shared_biases_first: float32 [2, 1152], replicated, may hold values from -384 to 384
- qkv_second: float32 [1152, 3, 1152], P('dp', None, 'tensor'), may hold values from 522.88 to 2092.8
- proj_second: float32 [1152, 1152], P(('tensor', 'dp')), may hold values from 20.928 to 83.648
- inner_second: float32 [1152, 4608], P('dp', 'tensor'), may hold values from 1105.92 to 4423.68
- outer_second: float32 [4608, 1152], P(('tensor', 'dp')), may hold values from 707.7888 to 2831.1553
- ada_second: float32 [6, 1152, 1152], P(None, 'tensor'), may hold values from 1966.08 to 7864.32
- head_biases_second: float32 [9, 1152], P(None, 'tensor'), may hold values from 2678.784 to 10706.944
- inner_bias_second: float32 [4608], P('tensor'), may hold values from 1105.92 to 4423.68
- shared_biases_second: float32 [2, 1152], replicated, may hold values from 2678.784 to 10706.944
Outputs:
- block_output: bfloat16 [8192, 1152], P(('dp', 'tensor'))
- input_grad: float32 [8192, 1152], P(('dp', 'tensor'))
- cond_grad: float32 [32, 1152], replicated
- qkv_updated: float32 [1152, 3, 1152], P('dp', None, 'tensor')
- proj_updated: float32 [1152, 1152], P(('tensor', 'dp'))
- inner_updated: float32 [1152, 4608], P('dp', 'tensor')
- outer_updated: float32 [4608, 1152], P(('tensor', 'dp'))
- ada_updated: float32 [6, 1152, 1152], P(None, 'tensor')
- head_biases_updated: float32 [9, 1152], P(None, 'tensor')
- inner_bias_updated: float32 [4608], P('tensor')
- shared_biases_updated: float32 [2, 1152], replicated
- qkv_first_new: float32 [1152, 3, 1152], P('dp', None, 'tensor')
- proj_first_new: float32 [1152, 1152], P(('tensor', 'dp'))
- inner_first_new: float32 [1152, 4608], P('dp', 'tensor')
- outer_first_new: float32 [4608, 1152], P(('tensor', 'dp'))
- ada_first_new: float32 [6, 1152, 1152], P(None, 'tensor')
- head_biases_first_new: float32 [9, 1152], P(None, 'tensor')
- inner_bias_first_new: float32 [4608], P('tensor')
- shared_biases_first_new: float32 [2, 1152], replicated
- qkv_second_new: float32 [1152, 3, 1152], P('dp', None, 'tensor')
- proj_second_new: float32 [1152, 1152], P(('tensor', 'dp'))
- inner_second_new: float32 [1152, 4608], P('dp', 'tensor')
- outer_second_new: float32 [4608, 1152], P(('tensor', 'dp'))
- ada_second_new: float32 [6, 1152, 1152], P(None, 'tensor')
- head_biases_second_new: float32 [9, 1152], P(None, 'tensor')
- inner_bias_second_new: float32 [4608], P('tensor')
- shared_biases_second_new: float32 [2, 1152], replicated
- qkv_copy: bfloat16 [1152, 3, 1152], P('dp', None, 'tensor')
- projection_bfloat_copy: bfloat16 [1152, 1152], P(('tensor', 'dp'))
- inner_copy: bfloat16 [1152, 4608], P('dp', 'tensor')
- outer_copy: bfloat16 [4608, 1152], P(('tensor', 'dp'))
Inputs may be any that keep to these rules, and one draw needn't show every extreme that they name: `segment_ids`: in each row segment numbers start at 0 and never fall; each of the 8 images holds at most 256 positions.
All inputs are finite; a program needn't handle non-finite values.
Results may differ from a plain program's by a relative error of at most 0.018.
The roundings to bfloat16 on the way count: a program that leaves them out, or rounds other values in their place, can miss the bound.
Values may be sent and summed in bfloat16 or wider, within the bound.
A program may use at most 256 MiB of HBM per device.

v0:
```python
import math

import jax
import jax.numpy as jnp
from jax import lax
from jax.sharding import PartitionSpec as P

HD = 72
STEP = 10


BETA_ONE = 0.5
BETA_TWO = 0.6
ADAM_EPS = 1e-08
DECAY = 0.01
NORM_EPSILON = 1e-06
RATES = (0.04, 0.3, 0.04, 0.04, 0.04, 0.4, 0.4, 0.4)
PRECISION_MAX = lax.Precision.HIGHEST
FLOAT = jnp.float32
HALF = jnp.bfloat16


def silu(values):
    return values / (1.0 + jnp.exp(-values))


def gelu_tanh(values):
    inner = math.sqrt(2.0 / math.pi) * (values + 0.044715 * values * values * values)
    return 0.5 * values * (1.0 + jnp.tanh(inner))


def normalize(values):
    centered = values - jnp.mean(values, axis=-1, keepdims=True)
    inv_std = lax.rsqrt(jnp.mean(centered * centered, axis=-1, keepdims=True) + NORM_EPSILON)
    return (centered * inv_std, inv_std)


def norm_back(grad_normed, normed, inv_std):
    first_mean = jnp.mean(grad_normed, axis=-1, keepdims=True)
    second_mean = jnp.mean(grad_normed * normed, axis=-1, keepdims=True)
    return inv_std * (grad_normed - first_mean - normed * second_mean)


def block_scores(query_block, keys, query_segs, key_segs):
    scores = jnp.einsum("qhe,khe->hqk", query_block, keys, preferred_element_type=FLOAT) * (
        1.0 / math.sqrt(HD)
    )
    same = query_segs[:, None] == key_segs[None, :]
    return jnp.where(same[None], scores, -1e30)


def attend_forward(row_qkv, row_segs):
    queries = row_qkv[:, 0]
    keys = row_qkv[:, 1]
    values = row_qkv[:, 2]
    length = queries.shape[0]
    heads_local = queries.shape[1]
    block = min(512, length)
    blocks = length // block

    def one_block(pieces):
        query_block, query_segs = pieces
        scores = block_scores(query_block, keys, query_segs, row_segs)
        top = jnp.max(scores, axis=-1, keepdims=True)
        expo = jnp.exp(scores - top)
        total = jnp.sum(expo, axis=-1, keepdims=True)
        probs = (expo / total).astype(HALF)
        attended = jnp.einsum("hqk,khe->qhe", probs, values, preferred_element_type=FLOAT)
        return (attended, (top + jnp.log(total))[:, :, 0])

    attended, log_totals = lax.map(
        one_block,
        (queries.reshape(blocks, block, heads_local, HD), row_segs.reshape(blocks, block)),
    )
    return (attended.reshape(length, heads_local, HD), log_totals)


def attend_backward(row_qkv, row_segs, grad_row, log_totals):
    queries = row_qkv[:, 0]
    keys = row_qkv[:, 1]
    values = row_qkv[:, 2]
    length = queries.shape[0]
    heads_local = queries.shape[1]
    block = min(512, length)
    blocks = length // block
    scale = 1.0 / math.sqrt(HD)

    def one_block(carry, pieces):
        key_sum, value_sum = carry
        query_block, query_segs, grad_block, block_total = pieces
        scores = block_scores(query_block, keys, query_segs, row_segs)
        probs = jnp.exp(scores - block_total[:, :, None])
        grad_probs = jnp.einsum("qhe,khe->hqk", grad_block, values, preferred_element_type=FLOAT)
        center = jnp.sum(probs * grad_probs, axis=-1, keepdims=True)
        grad_scores = (probs * (grad_probs - center)).astype(HALF)
        grad_query = (
            jnp.einsum("hqk,khe->qhe", grad_scores, keys, preferred_element_type=FLOAT) * scale
        )
        key_sum = (
            key_sum
            + jnp.einsum("hqk,qhe->khe", grad_scores, query_block, preferred_element_type=FLOAT)
            * scale
        )
        value_sum = value_sum + jnp.einsum(
            "hqk,qhe->khe", probs.astype(HALF), grad_block, preferred_element_type=FLOAT
        )
        return ((key_sum, value_sum), grad_query)

    zeros = jnp.zeros((length, heads_local, HD), FLOAT)
    sums, grad_queries = lax.scan(
        one_block,
        (zeros, zeros),
        (
            queries.reshape(blocks, block, heads_local, HD),
            row_segs.reshape(blocks, block),
            grad_row.reshape(blocks, block, heads_local, HD),
            log_totals,
        ),
    )
    return jnp.stack([grad_queries.reshape(length, heads_local, HD), sums[0], sums[1]], axis=1)


def adam_update(weight, grad, first, second, rate):
    first_new = BETA_ONE * first + (1.0 - BETA_ONE) * grad
    second_new = BETA_TWO * second + (1.0 - BETA_TWO) * grad * grad
    fix_one = 1.0 - BETA_ONE**STEP
    fix_two = 1.0 - BETA_TWO**STEP
    update = first_new / fix_one / (jnp.sqrt(second_new / fix_two) + ADAM_EPS)
    return (weight - rate * (update + DECAY * weight), first_new, second_new)


def on_device(
    block_input,
    conditions,
    segment_ids,
    segment_cond,
    cotangent,
    qkv_weight,
    proj_weight,
    inner_weight,
    outer_weight,
    ada_weight,
    head_biases,
    inner_bias,
    shared_biases,
    qkv_first,
    proj_first,
    inner_first,
    outer_first,
    ada_first,
    head_biases_first,
    inner_bias_first,
    shared_biases_first,
    qkv_second,
    proj_second,
    inner_second,
    outer_second,
    ada_second,
    head_biases_second,
    inner_bias_second,
    shared_biases_second,
):
    columns = qkv_weight.shape[2]
    heads_local = columns // HD
    rows_local = segment_ids.shape[0]
    row_length = segment_ids.shape[1]
    token_count = rows_local * row_length
    seg_count = segment_cond.shape[1]
    width = block_input.shape[1]
    share_count = token_count // lax.axis_size("tensor")
    share_start = lax.axis_index("tensor") * share_count

    def share(values):
        return lax.dynamic_slice_in_dim(values, share_start, share_count, 0)

    qkv_full, proj_full, inner_full, outer_full = (
        lax.all_gather(qkv_weight.astype(HALF), "dp", axis=0, tiled=True),
        lax.all_gather(proj_weight.astype(HALF), "dp", axis=0, tiled=True),
        lax.all_gather(inner_weight.astype(HALF), "dp", axis=0, tiled=True),
        lax.all_gather(outer_weight.astype(HALF), "dp", axis=0, tiled=True),
    )
    condition_select = (
        segment_cond[:, :, None] == jnp.arange(conditions.shape[0])[None, None, :]
    ).astype(FLOAT)
    condition_row_block = jnp.einsum(
        "btu,ua->bta", condition_select, conditions, precision=PRECISION_MAX
    )
    cond_act, silu_back = jax.vjp(silu, condition_row_block)
    local_mod = (
        jnp.einsum("rsd,kcd->rskc", cond_act, ada_weight, precision=PRECISION_MAX)
        + head_biases[3:][None, None]
    )
    full_mod = lax.all_gather(local_mod, "tensor", axis=3, tiled=True)
    seg_pick = (segment_ids[:, :, None] == jnp.arange(seg_count)[None, None, :]).astype(FLOAT)
    token_mod = jnp.einsum("rls,rskd->rlkd", seg_pick, full_mod, precision=PRECISION_MAX).reshape(
        token_count, 6, width
    )
    inputs = block_input.astype(FLOAT)
    normed_one, inv_one = normalize(inputs)
    hidden_one = (normed_one * (1.0 + token_mod[:, 1]) + token_mod[:, 0]).astype(HALF)
    qkv_values = (
        jnp.einsum("nd,dkc->nkc", hidden_one, qkv_full, preferred_element_type=FLOAT)
        + head_biases[:3][None]
    ).astype(HALF)
    row_qkv = qkv_values.reshape(rows_local, row_length, 3, heads_local, HD)
    row = 0
    attended_row, total_row = attend_forward(row_qkv[row], segment_ids[row])
    attended_rows = [attended_row]
    total_rows = [total_row]
    attended = jnp.stack(attended_rows).reshape(token_count, columns).astype(HALF)
    attn_partial = jnp.dot(attended, proj_full, preferred_element_type=FLOAT)
    branch_one = lax.psum(attn_partial, "tensor") + shared_biases[0]
    middle = inputs + token_mod[:, 2] * branch_one
    normed_two, inv_two = normalize(middle)
    hidden_two = (normed_two * (1.0 + token_mod[:, 4]) + token_mod[:, 3]).astype(HALF)
    pre_act = jnp.dot(hidden_two, inner_full, preferred_element_type=FLOAT) + inner_bias
    act_values, gelu_back = jax.vjp(gelu_tanh, pre_act)
    act_low = act_values.astype(HALF)
    ff_partial = jnp.dot(act_low, outer_full, preferred_element_type=FLOAT)
    branch_two = lax.psum(ff_partial, "tensor") + shared_biases[1]
    output = middle + token_mod[:, 5] * branch_two
    grad_out = cotangent.astype(FLOAT)
    grad_two = (grad_out * token_mod[:, 5]).astype(HALF)
    outer_grad = jnp.einsum("nf,nd->fd", act_low, grad_two, preferred_element_type=FLOAT)
    grad_act = jnp.einsum("nd,fd->nf", grad_two, outer_full, preferred_element_type=FLOAT)
    grad_pre = gelu_back(grad_act)[0].astype(HALF)
    inner_grad = jnp.einsum("nd,nf->df", hidden_two, grad_pre, preferred_element_type=FLOAT)
    back_two_partial = jnp.einsum("nf,df->nd", grad_pre, inner_full, preferred_element_type=FLOAT)
    grad_hidden_two = lax.psum(back_two_partial, "tensor")
    grad_middle = grad_out + norm_back(
        grad_hidden_two * (1.0 + token_mod[:, 4]), normed_two, inv_two
    )
    grad_one = (grad_middle * token_mod[:, 2]).astype(HALF)
    proj_grad = jnp.einsum("nc,nd->cd", attended, grad_one, preferred_element_type=FLOAT)
    grad_attended = jnp.einsum(
        "nd,cd->nc", grad_one, proj_full, preferred_element_type=FLOAT
    ).astype(HALF)
    grad_rows = grad_attended.reshape(rows_local, row_length, heads_local, HD)
    row = 0
    grad_qkv_rows = [
        attend_backward(row_qkv[row], segment_ids[row], grad_rows[row], total_rows[row])
    ]
    grad_qkv = jnp.stack(grad_qkv_rows).reshape(token_count, 3, columns).astype(HALF)
    qkv_grad = jnp.einsum("nd,nkc->dkc", hidden_one, grad_qkv, preferred_element_type=FLOAT)
    back_one_partial = jnp.einsum("nkc,dkc->nd", grad_qkv, qkv_full, preferred_element_type=FLOAT)
    grad_hidden_one = lax.psum(back_one_partial, "tensor")
    grad_input = grad_middle + norm_back(
        grad_hidden_one * (1.0 + token_mod[:, 1]), normed_one, inv_one
    )
    offset = lax.axis_index("tensor") * columns

    def local_columns(values):
        return lax.dynamic_slice_in_dim(values, offset, columns, 1)

    hidden_one_local = local_columns(grad_hidden_one)
    hidden_two_local = local_columns(grad_hidden_two)
    token_contributions = jnp.stack(
        [
            hidden_one_local,
            hidden_one_local * local_columns(normed_one),
            local_columns(grad_middle) * local_columns(branch_one),
            hidden_two_local,
            hidden_two_local * local_columns(normed_two),
            local_columns(grad_out) * local_columns(branch_two),
        ],
        axis=1,
    ).reshape(rows_local, row_length, 6, columns)
    grad_mod = jnp.einsum("rls,rlkc->rskc", seg_pick, token_contributions, precision=PRECISION_MAX)
    block_out = share(output).astype(HALF)
    input_out = share(grad_input)
    grad_cond_act = jnp.einsum("rskc,kcd->rsd", grad_mod, ada_weight, precision=PRECISION_MAX)
    gradient_condition_rows = silu_back(grad_cond_act)[0]
    condition_portion = jnp.einsum(
        "tko,tkc->oc", condition_select, gradient_condition_rows, precision=PRECISION_MAX
    )
    cond_grad = lax.psum(condition_portion, ("dp", "tensor"))
    head_bias_grad = jnp.concatenate(
        [jnp.sum(grad_qkv.astype(FLOAT), axis=0), jnp.sum(grad_mod, axis=(0, 1))], axis=0
    )
    inner_bias_grad = jnp.sum(grad_pre.astype(FLOAT), axis=0)
    shared_bias_grad = jnp.stack(
        [jnp.sum(grad_one.astype(FLOAT), axis=0), jnp.sum(grad_two.astype(FLOAT), axis=0)]
    )
    ada_grad = jnp.einsum("rsd,rskc->kcd", cond_act, grad_mod, precision=PRECISION_MAX)
    ada_total, head_total, inner_bias_total, shared_total = lax.psum(
        (ada_grad, head_bias_grad, inner_bias_grad, shared_bias_grad), "dp"
    )
    qkv_shard, proj_shard, inner_shard, outer_shard = (
        lax.psum_scatter(qkv_grad, "dp", scatter_dimension=0, tiled=True),
        lax.psum_scatter(proj_grad, "dp", scatter_dimension=0, tiled=True),
        lax.psum_scatter(inner_grad, "dp", scatter_dimension=0, tiled=True),
        lax.psum_scatter(outer_grad, "dp", scatter_dimension=0, tiled=True),
    )
    qkv_new = adam_update(qkv_weight, qkv_shard, qkv_first, qkv_second, RATES[0])
    proj_new = adam_update(proj_weight, proj_shard, proj_first, proj_second, RATES[1])
    inner_new = adam_update(inner_weight, inner_shard, inner_first, inner_second, RATES[2])
    outer_new = adam_update(outer_weight, outer_shard, outer_first, outer_second, RATES[3])
    ada_new = adam_update(ada_weight, ada_total, ada_first, ada_second, RATES[4])
    head_new = adam_update(head_biases, head_total, head_biases_first, head_biases_second, RATES[5])
    inner_bias_new = adam_update(
        inner_bias, inner_bias_total, inner_bias_first, inner_bias_second, RATES[6]
    )
    shared_new = adam_update(
        shared_biases, shared_total, shared_biases_first, shared_biases_second, RATES[7]
    )
    return (
        block_out,
        input_out,
        cond_grad,
        qkv_new[0],
        proj_new[0],
        inner_new[0],
        outer_new[0],
        ada_new[0],
        head_new[0],
        inner_bias_new[0],
        shared_new[0],
        qkv_new[1],
        proj_new[1],
        inner_new[1],
        outer_new[1],
        ada_new[1],
        head_new[1],
        inner_bias_new[1],
        shared_new[1],
        qkv_new[2],
        proj_new[2],
        inner_new[2],
        outer_new[2],
        ada_new[2],
        head_new[2],
        inner_bias_new[2],
        shared_new[2],
        qkv_new[0].astype(HALF),
        proj_new[0].astype(HALF),
        inner_new[0].astype(HALF),
        outer_new[0].astype(HALF),
    )


def solution(mesh):
    in_specs = (
        P("dp", None),
        P(),
        P("dp", None),
        P("dp", None),
        P("dp", None),
        P("dp", None, "tensor"),
        P(("tensor", "dp"), None),
        P("dp", "tensor"),
        P(("tensor", "dp"), None),
        P(None, "tensor", None),
        P(None, "tensor"),
        P("tensor"),
        P(),
        P("dp", None, "tensor"),
        P(("tensor", "dp"), None),
        P("dp", "tensor"),
        P(("tensor", "dp"), None),
        P(None, "tensor", None),
        P(None, "tensor"),
        P("tensor"),
        P(),
        P("dp", None, "tensor"),
        P(("tensor", "dp"), None),
        P("dp", "tensor"),
        P(("tensor", "dp"), None),
        P(None, "tensor", None),
        P(None, "tensor"),
        P("tensor"),
        P(),
    )
    out_specs = (
        P(("dp", "tensor"), None),
        P(("dp", "tensor"), None),
        P(),
        P("dp", None, "tensor"),
        P(("tensor", "dp"), None),
        P("dp", "tensor"),
        P(("tensor", "dp"), None),
        P(None, "tensor", None),
        P(None, "tensor"),
        P("tensor"),
        P(),
        P("dp", None, "tensor"),
        P(("tensor", "dp"), None),
        P("dp", "tensor"),
        P(("tensor", "dp"), None),
        P(None, "tensor", None),
        P(None, "tensor"),
        P("tensor"),
        P(),
        P("dp", None, "tensor"),
        P(("tensor", "dp"), None),
        P("dp", "tensor"),
        P(("tensor", "dp"), None),
        P(None, "tensor", None),
        P(None, "tensor"),
        P("tensor"),
        P(),
        P("dp", None, "tensor"),
        P(("tensor", "dp"), None),
        P("dp", "tensor"),
        P(("tensor", "dp"), None),
    )
    return jax.shard_map(
        on_device, mesh=mesh, in_specs=in_specs, out_specs=out_specs, check_vma=False
    )
```

profile of v0, /device:TPU:0, one launch (start us, length us, event | category | flops | bytes accessed | tf_op | source)
XLA Modules:
  0.0 1476.4 jit_solution(12935331074179732440)
XLA Ops:
  10.9 9.7 convolution_add_fusion.1
  21.1 32.0 %all-gather = f32[8,6,1152]{1,0,2:T(8,128)} all-gather(f32[8,6,288]{1,0,2:T(8,128)S(1)} %copy.71), channel_id=2, replica_groups=mesh['dp'=8,'tensor'=4] {'tensor'}, dimensions={2}, use_global_device_ids=true | all-gather | bytes 276480 | tf_op jit(solution)/shard_map/all_gather | solution.py:193
  58.0 35.4 %all-gather.1 = bf16[8,36,1152]{2,1,0:T(8,128)(2,1)} all-gather(bf16[1,36,1152]{2,1,0:T(8,128)(2,1)S(1)} %convert_bitcast_fusion), channel_id=1, replica_groups=mesh['dp'=8,'tensor'=4] {'dp'}, dimensions={0}, use_global_device_ids=true | all-gather | bytes 746496 | tf_op jit(solution)/shard_map/all_gather | solution.py:178
  96.6 14.8 %fusion.85 = f32[1024,6,1152]{2,0,1:T(8,128)} fusion(f32[8,6,1152]{2,0,1:T(8,128)S(1)} %copy.72, s32[1024]{0:T(1024)S(1)} %bitcast.247), kind=kOutput, calls=%fused_computation.161 | convolution fusion | flops 679485440 | bytes 28536832 | tf_op jit(solution)/shard_map/rls,rskd->rlkd/dot_general | solution.py:195
  126.0 17.6 %while.27 = (s32[]{:T(128)}, bf16[2,512,4,72]{1,3,2,0:T(8,128)(2,1)}, f32[2,4,512]{2,1,0:T(4,128)}, s32[2,512]{1,0:T(2,128)S(1)}, s32[1,1024]{1,0:T(1,128)S(1)},...) while((s32[]{:T(128)}, ...), condition=%wide.region_5.6_spmd, body=%wide.region_2.5_spmd.sunk | while | flops 629667840 | bytes 36612352 | solution.py:71
  154.3 91.4 %all-reduce.10.cloned.1.call-done = f32[1024,1152]{1,0:T(8,128)} async-done(((f32[1024,1152]{1,0:T(8,128)}), f32[1024,1152]{1,0:T(8,128)}) %all-reduce.10.cloned.1.call-update) | async-done | bytes 4718608 | tf_op jit(solution)/shard_map/psum | solution.py:212
  255.9 20.1 %convert_reduce_fusion.1 = (f32[1152]{0:T(1024)}, bf16[1024,1152]{1,0:T(8,128)(2,1)}, bf16[1024,1152]{1,0:T(8,128)(2,1)S(1)}, f32[1024,1152]{1,0:T(8,128)}) fusion(f32[1024,6,1152]{2,0,1:T(8,128)} %fusion.85, bf16[1024,1152]{1,0:T(8,128)(2,1)S(1)} %copy-done.11, f32[1024]{0:T(1024)S(1)} %add_rsqrt_fusion, f32[1024,1152]{1,0:T(8,128)S(1)} %get-tuple-element.303, ...), kind=kLoop, calls=%fused_computation.81 | loop fusion | flops 12974976 | bytes 30683648 | tf_op jit(solution)/shard_map/reduce_sum | solution.py:282
  276.0 27.6 %all-gather.8.cloned.1.call-done = bf16[1152,1152]{1,0:T(8,128)(2,1)} async-done(((bf16[144,1152]{1,0:T(8,128)(2,1)}), bf16[1152,1152]{1,0:T(8,128)(2,1)}) %all-gather.8.cloned.1.call-update) | async-done | bytes 2654224 | tf_op jit(solution)/shard_map/all_gather | solution.py:179
  317.4 102.9 %reduce-scatter.10.cloned.1.call-done = f32[144,1152]{1,0:T(8,128)} async-done(((f32[1152,1152]{1,0:T(8,128)}), f32[144,1152]{1,0:T(8,128)}) %reduce-scatter.10.cloned.1.call-update) | async-done | bytes 663568 | tf_op jit(solution)/shard_map/reduce_scatter | solution.py:292
  424.4 54.9 %all-gather.10.cloned.1.call-done = bf16[1152,1152]{1,0:T(8,128)(2,1)} async-done(((bf16[144,1152]{1,0:T(8,128)(2,1)}), bf16[1152,1152]{1,0:T(8,128)(2,1)}) %all-gather.10.cloned.1.call-update) | async-done | bytes 2654224 | tf_op jit(solution)/shard_map/all_gather | solution.py:180
  479.3 9.5 convert_reduce_fusion.3
  495.5 9.6 fusion.105
  505.1 83.1 %all-reduce.12.cloned.1.call-done = f32[1024,1152]{1,0:T(8,128)} async-done(((f32[1024,1152]{1,0:T(8,128)}), f32[1024,1152]{1,0:T(8,128)}) %all-reduce.12.cloned.1.call-update) | async-done | bytes 4718608 | tf_op jit(solution)/shard_map/psum | solution.py:229
  595.4 8.6 convert_reduce_fusion.2
  612.8 40.1 %while.28 = (s32[]{:T(128)}, f32[1024,4,72]{0,2,1:T(8,128)S(1)}, f32[1024,4,72]{0,2,1:T(8,128)}, bf16[2,512,4,72]{1,3,2,0:T(8,128)(2,1)}, bf16[2,512,4,72]{1,3,2...) while((s32[]{:T(128)}, f32[1024,4,72]{0,2,1:T(8,128)S(1)}, ...), condition=%wide.region_15.16_spmd.clone, body=%wide.region_13.15_spmd.clone.sunk | while | flops 1543550976 | bytes 166660464 | solution.py:110
  664.0 7.3 fusion.102
  684.8 149.6 %all-reduce.18.cloned.1.call-done = (f32[1024,1152]{1,0:T(8,128)}, f32[1024,1152]{1,0:T(8,128)}) async-done(((f32[1024,1152]{1,0:T(8,128)}, f32[1024,1152]{1,0:T(8,128)}), (f32[1024,1152]{1,0:T(8,128)}, f32[1024,1152]{1,0:T(8,128)})) %all-reduce.18.cloned.1.call-update) | async-done | bytes 9437200 | tf_op jit(solution)/shard_map/psum | solution.py:220
  862.1 8.6 fusion.70
  880.1 53.9 %fusion = f32[48,1152]{1,0:T(8,128)S(1)} fusion(f32[288,1152]{1,0:T(8,128)} %fusion.127), kind=kCustom, calls=%all-reduce-scatter | all-reduce-scatter fusion | flops 442369 | bytes 1548800
  952.3 45.7 %all-reduce.2 = (f32[9,288]{1,0:T(8,128)S(1)}, f32[1152]{0:T(1024)S(1)}, f32[2,1152]{1,0:T(2,128)S(1)}) all-reduce(f32[9,288]{1,0:T(8,128)S(1)} %pad_maximum_fusion.1, f32[1152]{0:T(1024)S(1)} %copy-done.66, f32[2,1152]{1,0:T(2,128)S(1)} %pad_maximum_fusion.2), channel_id=1, replica_groups=mesh['dp'=8,'tensor'=4] {'dp'}, use_global_device_ids=true, to_apply=%region_27.28 | all-reduce | flops 6048 | bytes 48384 | tf_op jit(solution)/shard_map/psum | solution.py:285
  1007.9 70.3 %reduce-scatter.8.cloned.1.call-done = f32[144,1152]{1,0:T(8,128)} async-done(((f32[1152,1152]{1,0:T(8,128)}), f32[144,1152]{1,0:T(8,128)}) %reduce-scatter.8.cloned.1.call-update) | async-done | bytes 663568 | tf_op jit(solution)/shard_map/reduce_scatter | solution.py:291
  1081.7 259.3 %all-reduce.16.cloned.1.call-done = f32[6,288,1152]{2,1,0:T(8,128)} async-done(((f32[6,288,1152]{2,1,0:T(8,128)}), f32[6,288,1152]{2,1,0:T(8,128)}) %all-reduce.16.cloned.1.call-update) | async-done | bytes 7962640 | tf_op jit(solution)/shard_map/psum | solution.py:285
  1341.0 20.2 %multiply_subtract_fusion = (f32[6,288,1152]{2,1,0:T(8,128)}, f32[6,288,1152]{2,1,0:T(8,128)}, f32[6,288,1152]{2,1,0:T(8,128)}) fusion(f32[6,288,1152]{2,1,0:T(8,128)} %param.42, f32[6,288,1152]{2,1,0:T(8,128)} %param.50, f32[6,288,1152]{2,1,0:T(8,128)} %all-reduce.16.cloned.1.call-done, f32[6,288,1152]{2,1,0:T(8,128)} %param.58), kind=kLoop, calls=%fused_computation.52 | loop fusion | flops 27869184 | bytes 55738368 | tf_op jit(solution)/shard_map/sub | solution.py:129
  1361.2 106.7 %all-reduce.14.cloned.1.call-done = f32[32,1152]{1,0:T(8,128)} async-done(((f32[32,1152]{1,0:T(8,128)}), f32[32,1152]{1,0:T(8,128)}) %all-reduce.14.cloned.1.call-update) | async-done | bytes 147472 | tf_op jit(solution)/shard_map/psum | solution.py:276
  (324 shorter events, 238.5 us)
Async XLA Ops:
  7.2 109.6 %all-gather.6.cloned.1.call-start = ((), (), s32[]{:S(2)}) async-start(), calls=%async_computation.3 | async-start | bytes 2985984 | tf_op jit(solution)/shard_map/all_gather | solution.py:177
  9.2 236.5 %all-reduce.10.cloned.1.call-start = ((), (), s32[]{:S(2)}) async-start(), calls=%async_computation.4 | async-start | bytes 9437184 | tf_op jit(solution)/shard_map/psum | solution.py:212
  150.9 152.7 %all-gather.8.cloned.1.call-start = ((), (), s32[]{:S(2)}) async-start(), calls=%async_computation.5 | async-start | bytes 2985984 | tf_op jit(solution)/shard_map/all_gather | solution.py:179
  152.9 267.5 %reduce-scatter.10.cloned.1.call-start = ((), (), s32[]{:S(2)}) async-start(), calls=%async_computation.11 | async-start | bytes 5971968 | tf_op jit(solution)/shard_map/reduce_scatter | solution.py:292
  317.4 161.9 %copy-start.27 = (bf16[1024,1152]{1,0:T(8,128)(2,1)S(1)}, bf16[1024,1152]{1,0:T(8,128)(2,1)}, u32[]{:S(2)}) copy-start(bf16[1024,1152]{1,0:T(8,128)(2,1)} %get-tuple-element.294) | copy-start | bytes 7077892
  317.4 161.9 %all-gather.10.cloned.1.call-start = ((), (), s32[]{:S(2)}) async-start(), calls=%async_computation.6 | async-start | bytes 2985984 | tf_op jit(solution)/shard_map/all_gather | solution.py:180
  424.3 163.8 %all-reduce.12.cloned.1.call-start = ((), (), s32[]{:S(2)}) async-start(), calls=%async_computation.7 | async-start | bytes 9437184 | tf_op jit(solution)/shard_map/psum | solution.py:229
  495.4 339.0 %all-reduce.18.cloned.1.call-start = ((), (), s32[]{:S(2)}) async-start(), calls=%async_computation.13 | async-start | bytes 18874368 | tf_op jit(solution)/shard_map/psum | solution.py:220
  663.9 340.9 %reduce-scatter.6.cloned.1.call-start = ((), (), s32[]{:S(2)}) async-start(), calls=%async_computation.9 | async-start | bytes 5971968 | tf_op jit(solution)/shard_map/reduce_scatter | solution.py:289
  671.3 406.9 %reduce-scatter.8.cloned.1.call-start = ((), (), s32[]{:S(2)}) async-start(), calls=%async_computation.10 | async-start | bytes 5971968 | tf_op jit(solution)/shard_map/reduce_scatter | solution.py:291
  680.3 660.7 %all-reduce.16.cloned.1.call-start = ((), (), s32[]{:S(2)}) async-start(), calls=%async_computation.12 | async-start | bytes 15925248 | tf_op jit(solution)/shard_map/psum | solution.py:285
  680.4 156.3 %copy-start.6 = (bf16[1024,1152]{1,0:T(8,128)(2,1)S(1)}, bf16[1024,1152]{1,0:T(8,128)(2,1)}, u32[]{:S(2)}) copy-start(bf16[1024,1152]{1,0:T(8,128)(2,1)} %param.33) | copy-start | bytes 7077892
  680.4 156.3 %copy-start.50 = (f32[1024]{0:T(1024)S(1)}, f32[1024]{0:T(1024)}, u32[]{:S(2)}) copy-start(f32[1024]{0:T(1024)} %copy-done.49) | copy-start | bytes 12292
  680.4 156.2 %copy-start.52 = (f32[1024]{0:T(1024)S(1)}, f32[1024]{0:T(1024)}, u32[]{:S(2)}) copy-start(f32[1024]{0:T(1024)} %copy-done.51) | copy-start | bytes 12292
  870.7 597.1 %all-reduce.14.cloned.1.call-start = ((), (), s32[]{:S(2)}) async-start(), calls=%async_computation.8 | async-start | bytes 294912 | tf_op jit(solution)/shard_map/psum | solution.py:276
  878.0 65.7 %copy-start.37 = (f32[36,1152]{1,0:T(8,128)S(1)}, f32[36,1152]{1,0:T(8,128)}, u32[]{:S(2)}) copy-start(f32[36,1152]{1,0:T(8,128)} %param.39) | copy-start | bytes 497668
  878.1 65.7 %copy-start.43 = (f32[36,1152]{1,0:T(8,128)S(1)}, f32[36,1152]{1,0:T(8,128)}, u32[]{:S(2)}) copy-start(f32[36,1152]{1,0:T(8,128)} %param.47) | copy-start | bytes 497668
  878.1 65.7 %copy-start.44 = (f32[36,1152]{1,0:T(8,128)S(1)}, f32[36,1152]{1,0:T(8,128)}, u32[]{:S(2)}) copy-start(f32[36,1152]{1,0:T(8,128)} %param.55) | copy-start | bytes 497668
  878.1 66.8 %copy-start.60 = (f32[1024]{0:T(1024)S(1)}, f32[1024]{0:T(1024)}, u32[]{:S(2)}) copy-start(f32[1024]{0:T(1024)} %get-tuple-element.226) | copy-start | bytes 12292
  878.1 66.9 %copy-start.59 = (f32[1024]{0:T(1024)S(1)}, f32[1024]{0:T(1024)}, u32[]{:S(2)}) copy-start(f32[1024]{0:T(1024)} %get-tuple-element.225) | copy-start | bytes 12292
  934.0 9.3 collective-permute-start
  938.4 4.9 collective-permute-start.1
  1000.0 78.2 %copy-start.21 = (f32[144,1152]{1,0:T(8,128)S(1)}, f32[144,1152]{1,0:T(8,128)}, u32[]{:S(2)}) copy-start(f32[144,1152]{1,0:T(8,128)} %param.40) | copy-start | bytes 1990660
  1341.0 128.5 %copy-start.1 = (f32[32,1152]{1,0:T(8,128)S(1)}, f32[32,1152]{1,0:T(8,128)}, u32[]{:S(2)}) copy-start(f32[32,1152]{1,0:T(8,128)} %param.34) | copy-start | bytes 442372
  (79 other events, 1325.8 us)
Sparse Core Ops, SparseCore 0:
  10.9 59.4 all-gather.5
  151.0 94.5 all-reduce.9
  248.4 55.1 all-gather.7
  317.5 102.7 reduce-scatter.9
  424.5 54.7 all-gather.9
  495.5 92.5 all-reduce.11
  664.0 170.3 all-reduce.17
  839.0 130.1 reduce-scatter.5
  973.4 104.7 reduce-scatter.7
  1082.9 257.9 all-reduce.15
  1348.0 119.7 all-reduce.13
where the time goes:
time: 1480 us
  waiting for transfers between devices  949 us (64%)
  blocking collectives  167 us (11%)
  matrix products  153 us (10%)
  other arithmetic  131 us (9%)
  local copies, waits for them, and re-layouts  53.5 us (4%)
  between operations  15.9 us (1%)
    psum x1, waiting for transfers between devices, on_device(): lax.psum((ada_grad, head_bias_grad, inner_bias_grad, shared_bias_grad), '...  259 us
    psum x1, waiting for transfers between devices, on_device(): branch_two = lax.psum(ff_partial, 'tensor') + shared_biases[1]  150 us
    psum x1, waiting for transfers between devices, on_device(): cond_grad = lax.psum(condition_portion, ('dp', 'tensor'))  107 us
    reduce_scatter x1, waiting for transfers between devices, on_device(): lax.psum_scatter(outer_grad, 'dp', scatter_dimension=0, tiled=True)  103 us
    psum x1, waiting for transfers between devices, on_device(): branch_one = lax.psum(attn_partial, 'tensor') + shared_biases[0]  91.4 us
    psum x1, waiting for transfers between devices, on_device(): grad_hidden_two = lax.psum(back_two_partial, 'tensor')  83.1 us
    reduce_scatter x1, waiting for transfers between devices, on_device(): lax.psum_scatter(inner_grad, 'dp', scatter_dimension=0, tiled=True)  70.3 us
    all_gather x1, waiting for transfers between devices, on_device(): lax.all_gather(outer_weight.astype(HALF), 'dp', axis=0, tiled=True)  54.9 us
  transfers between devices with their start and end apart: 13, of which 10 were waited for; matrix products, arithmetic and copies ran while one was open for 16% of the time, Pallas kernels for 0%

commit v1 on v0

--- a/solution.py
+++ b/solution.py
@@ -1,8 +1,11 @@
+import functools
 import math
 
 import jax
 import jax.numpy as jnp
 from jax import lax
+from jax.experimental import pallas as pl
+from jax.experimental.pallas import tpu as pltpu
 from jax.sharding import PartitionSpec as P
 
 HD = 72
@@ -129,7 +132,532 @@
     return (weight - rate * (update + DECAY * weight), first_new, second_new)
 
 
-def on_device(
+def sum_to_shares(partial):
+    return lax.psum_scatter(
+        partial.astype(HALF), "tensor", scatter_dimension=0, tiled=True
+    ).astype(FLOAT)
+
+
+def sum_to_owners(partial):
+    return lax.psum_scatter(
+        partial.astype(HALF), "dp", scatter_dimension=0, tiled=True
+    ).astype(FLOAT)
+
+
+SEG_MOST = 256
+CORES = 2
+MESH = pl.DeviceIdType.MESH
+NT_DIMS = (((1,), (1,)), ((), ()))
+TN_DIMS = (((0,), (0,)), ((), ()))
+VMEM_BYTES = 60 * 1024 * 1024
+
+
+def line_length(count):
+    length = 1
+    while (2 * length) ** 2 <= count:
+        length *= 2
+    return length
+
+
+def mm(left, right):
+    return jnp.dot(left, right, preferred_element_type=FLOAT)
+
+
+def mm_nt(left, right):
+    return lax.dot_general(left, right, NT_DIMS, preferred_element_type=FLOAT)
+
+
+def mm_tn(left, right):
+    return lax.dot_general(left, right, TN_DIMS, preferred_element_type=FLOAT)
+
+
+def split_two(values):
+    high = values.astype(HALF)
+    return high, (values - high.astype(FLOAT)).astype(HALF)
+
+
+class Place:
+    def __init__(self, dp_count, tensor_count):
+        self.dp_count, self.tensor_count = dp_count, tensor_count
+        self.xs = line_length(dp_count)
+        self.zs = dp_count // self.xs
+        self.ys = tensor_count // CORES
+        self.dp, self.tensor = lax.axis_index("dp"), lax.axis_index("tensor")
+        self.z, self.x = lax.div(self.dp, self.xs), lax.rem(self.dp, self.xs)
+        self.y, self.core = lax.div(self.tensor, CORES), lax.rem(self.tensor, CORES)
+
+    def z_of(self, step):
+        return lax.rem(self.z + step + self.zs, self.zs)
+
+    def x_of(self, step):
+        return lax.rem(self.x + step + self.xs, self.xs)
+
+    def z_peer(self, step):
+        return (self.z_of(step) * self.xs + self.x, self.tensor)
+
+    def x_peer(self, step):
+        return (self.z * self.xs + self.x_of(step), self.tensor)
+
+    def tensor_peer(self, step):
+        return (self.dp, lax.rem(self.tensor + step, self.tensor_count))
+
+    def core_peer(self):
+        return (self.dp, self.y * CORES + 1 - self.core)
+
+    def y_peer(self):
+        return (self.dp, (1 - self.y) * CORES + self.core)
+
+    def share_of(self, other_y, other_core):
+        y = 1 - self.y if other_y else self.y
+        core = 1 - self.core if other_core else self.core
+        return y * CORES + core
+
+
+def greet(peers):
+    barrier = pltpu.get_barrier_semaphore()
+    for peer in peers:
+        pl.semaphore_signal(barrier, inc=1, device_id=peer, device_id_type=MESH)
+    pl.semaphore_wait(barrier, len(peers))
+
+
+def remote(src, dst, sends, recvs, peer):
+    return pltpu.make_async_remote_copy(
+        src_ref=src, dst_ref=dst, send_sem=sends, recv_sem=recvs, device_id=peer, device_id_type=MESH
+    )
+
+
+def rows_at(start, count):
+    return pl.ds(pl.multiple_of(start, 16), count)
+
+
+class Gather:
+    def __init__(self, place, pieces, z_sems, x_sems):
+        self.place, self.pieces = place, pieces
+        self.z_send, self.z_recv = z_sems
+        self.x_send, self.x_recv = x_sems
+        self.pending = []
+
+    def slot(self, piece, z, x):
+        own, full, shard_rows, first, count = self.pieces[piece]
+        return full.at[rows_at((z * self.place.xs + x) * shard_rows + first, count)]
+
+    def z_copy(self, piece, step):
+        own, full, shard_rows, first, count = self.pieces[piece]
+        at = self.place
+        return remote(
+            own.at[pl.ds(first, count)], self.slot(piece, at.z, at.x),
+            self.z_send.at[piece, step - 1], self.z_recv.at[piece, step - 1], at.z_peer(step),
+        )
+
+    def z_landing(self, piece, step):
+        at = self.place
+        landed = self.slot(piece, at.z_of(-step), at.x)
+        return remote(
+            landed, landed, self.z_send.at[piece, step - 1], self.z_recv.at[piece, step - 1], at.z_peer(step)
+        )
+
+    def x_copy(self, piece, back, step):
+        at = self.place
+        chunk = self.slot(piece, at.z_of(-back), at.x)
+        source = chunk
+        if back == 0:
+            own, full, shard_rows, first, count = self.pieces[piece]
+            source = own.at[pl.ds(first, count)]
+        return remote(
+            source, chunk, self.x_send.at[piece, back, step - 1], self.x_recv.at[piece, back, step - 1],
+            at.x_peer(step),
+        )
+
+    def x_landing(self, piece, back, step):
+        at = self.place
+        landed = self.slot(piece, at.z_of(-back), at.x_of(-step))
+        return remote(
+            landed, landed, self.x_send.at[piece, back, step - 1], self.x_recv.at[piece, back, step - 1],
+            at.x_peer(step),
+        )
+
+    def start(self, piece):
+        at = self.place
+        for step in sorted(range(1, at.zs), key=lambda s: -min(s, at.zs - s)):
+            self.z_copy(piece, step).start()
+        for step in range(1, at.xs):
+            self.x_copy(piece, 0, step).start()
+
+    def sent(self, piece):
+        for step in range(1, self.place.zs):
+            self.z_copy(piece, step).wait_send()
+
+    def forward(self, piece):
+        at = self.place
+        for back in range(1, at.zs):
+            self.z_landing(piece, back).wait_recv()
+            for step in range(1, at.xs):
+                self.x_copy(piece, back, step).start()
+
+    def arrive(self, piece):
+        at = self.place
+        for back in range(at.zs):
+            for step in range(1, at.xs):
+                self.x_landing(piece, back, step).wait_recv()
+
+    def finish(self, piece):
+        at = self.place
+        for back in range(at.zs):
+            for step in range(1, at.xs):
+                self.x_copy(piece, back, step).wait_send()
+
+
+def layer_norm(values):
+    mean = jnp.mean(values, axis=-1, keepdims=True)
+    centered = values - mean
+    inv_std = lax.rsqrt(jnp.mean(centered * centered, axis=-1, keepdims=True) + NORM_EPSILON)
+    return centered * inv_std, inv_std
+
+
+def forward_kernel(
+    sizes,
+    x_ref, seg_col, seg_row, cond_ref, ada_ref, mod_bias, qkv_bias, inner_bias, shared_bias,
+    proj_place, wq, wp, wi, wo,
+    wq_out, wp_out, wi_out, wo_out, hid_a_out, heads_out, lse_out, att_out, hid_b_out, act_out,
+    slope_out, part_out, branch_out, middle_out, modk_out,
+    wq_full, wp_full, wp_tight, wi_full, wo_full, hid_a, heads, lse, att_heads, att, part, core_in,
+    y_out, y_in, hid_b, act, slope, ff_part, branch, middle, modk, mods, ada_tile,
+    z_send, z_recv, x_send, x_recv, mod_send, mod_recv, sum_send, sum_recv, gat_send, gat_recv,
+    ada_sem, save_sem,
+):
+    at = Place(sizes["dp"], sizes["tensor"])
+    tokens, width, columns, share = sizes["tokens"], sizes["width"], sizes["columns"], sizes["share"]
+    nheads, segs = columns // HD, cond_ref.shape[0]
+    window = min(tokens, share + 2 * SEG_MOST)
+    greet(
+        [at.z_peer(s) for s in range(1, at.zs)]
+        + [at.x_peer(s) for s in range(1, at.xs)]
+        + [at.tensor_peer(s) for s in range(1, at.tensor_count)]
+    )
+    pieces = []
+    for own, full in ((wq, wq_full), (wp, wp_full), (wi, wi_full), (wo, wo_full)):
+        shard = own.shape[0]
+        unit = 48 if shard % 48 == 0 else shard
+        pieces += [(own, full, shard, first, unit) for first in range(0, shard, unit)]
+    gather = Gather(at, pieces, (z_send, z_recv), (x_send, x_recv))
+    n_q, n_p, n_i = (wq.shape[0] // 48 if wq.shape[0] % 48 == 0 else 1), 1, (wi.shape[0] // 48 if wi.shape[0] % 48 == 0 else 1)
+    list_q, list_p = list(range(n_q)), [n_q]
+    list_i = list(range(n_q + n_p, n_q + n_p + n_i))
+    list_o = list(range(n_q + n_p + n_i, len(pieces)))
+    last = len(pieces)
+    started = [0]
+
+    def push():
+        piece = started[0]
+        if piece < last:
+            if piece >= 2:
+                gather.sent(piece - 2)
+            gather.start(piece)
+            started[0] += 1
+
+    push()
+    push()
+
+    for own, full in ((wq, wq_full), (wp, wp_full), (wi, wi_full), (wo, wo_full)):
+        full[rows_at(at.dp * own.shape[0], own.shape[0]), :] = own[...]
+
+    def ada_copy(group):
+        return pltpu.make_async_copy(ada_ref.at[group], ada_tile.at[group % 2], ada_sem.at[group % 2])
+
+    ada_copy(0).start()
+    cond_high, cond_low = split_two(cond_ref[...])
+    cond_both = jnp.concatenate([cond_high, cond_low], axis=0)
+    for group in range(6):
+        if group < 5:
+            ada_copy(group + 1).start()
+        ada_copy(group).wait()
+        weight_high, weight_low = split_two(ada_tile[group % 2])
+        both = mm_nt(cond_both, weight_high)
+        mods[at.tensor, group] = (
+            both[:segs] + both[segs:] + mm_nt(cond_high, weight_low) + mod_bias[group]
+        )
+
+    def mod_copy(step):
+        own = mods.at[at.tensor]
+        return remote(own, own, mod_send.at[step - 1], mod_recv.at[step - 1], at.tensor_peer(step))
+
+    def mod_landing(step):
+        landed = mods.at[lax.rem(at.tensor + at.tensor_count - step, at.tensor_count)]
+        return remote(landed, landed, mod_send.at[step - 1], mod_recv.at[step - 1], at.tensor_peer(step))
+
+    for step in range(1, at.tensor_count):
+        mod_copy(step).start()
+    for step in range(1, at.tensor_count):
+        mod_landing(step).wait_recv()
+    for group in range(6):
+        whole = jnp.concatenate([mods[t, group] for t in range(at.tensor_count)], axis=1)
+        high, low = split_two(whole)
+        modk[group] = jnp.concatenate([high, low], axis=0)
+
+    def pick(rows):
+        ids = seg_col[rows, :]
+        lanes = lax.broadcasted_iota(jnp.int32, (1, 2 * segs), 1)
+        return (ids == lax.rem(lanes, segs)).astype(FLOAT).astype(HALF)
+
+    gather.forward(0)
+    push()
+
+    def hidden_block(index, carry):
+        rows = rows_at(index * share, share)
+        normed, _ = layer_norm(x_ref[rows, :].astype(FLOAT))
+        chosen = pick(rows)
+        hid_a[rows, :] = (normed * (1.0 + mm(chosen, modk[1])) + mm(chosen, modk[0])).astype(HALF)
+        return carry
+
+    lax.fori_loop(0, tokens // share, hidden_block, 0)
+    for piece in list_q[1:]:
+        gather.forward(piece)
+        push()
+    for piece in list_q:
+        gather.arrive(piece)
+    gather.forward(list_p[0])
+    push()
+
+    def qkv_block(index, carry):
+        rows = rows_at(index * share, share)
+        values = mm(hid_a[rows, :], wq_full[...]) + qkv_bias[...]
+        for head in range(3 * nheads):
+            heads[head, rows, :] = values[:, head * HD:(head + 1) * HD].astype(HALF)
+        return carry
+
+    lax.fori_loop(0, tokens // share, qkv_block, 0)
+
+    def attend(block):
+        start = block * share
+        rows = rows_at(start, share)
+        first = pl.multiple_of(jnp.clip(start - SEG_MOST, 0, tokens - window), 128)
+        keys = pl.ds(first, window)
+
+        def one_head(head, carry):
+            same = seg_col[rows, :] == seg_row[:, keys]
+            scores = mm_nt(heads[head, rows, :], heads[nheads + head, keys, :]) * (1.0 / math.sqrt(HD))
+            scores = jnp.where(same, scores, -1e30)
+            top = jnp.max(scores, axis=-1, keepdims=True)
+            expo = jnp.exp(scores - top)
+            total = jnp.sum(expo, axis=-1, keepdims=True)
+            probs = (expo * (1.0 / total)).astype(HALF)
+            att_heads[head, :, :] = mm(probs, heads[2 * nheads + head, keys, :])
+            lse[head, rows, :] = top + jnp.log(total)
+            return carry
+
+        lax.fori_loop(0, nheads, one_head, 0)
+        joined = jnp.concatenate([att_heads[head] for head in range(nheads)], axis=1).astype(HALF)
+        att[rows, :] = joined
+        return joined
+
+    def core_copy(slot, src):
+        return remote(src, core_in.at[slot], sum_send.at[slot], sum_recv.at[slot], at.core_peer())
+
+    y_copy = remote(y_out, y_in, sum_send.at[2], sum_recv.at[2], at.y_peer())
+
+    joined = attend(at.share_of(True, True))
+    gather.arrive(list_p[0])
+    wp_tight[...] = mm(proj_place[...], wp_full[...]).astype(HALF)
+    part[0] = mm(joined, wp_tight[...]).astype(HALF)
+    core_copy(0, part.at[0]).start()
+    gather.forward(list_i[0])
+    push()
+    joined = attend(at.share_of(False, True))
+    part[1] = mm(joined, wp_tight[...]).astype(HALF)
+    core_copy(1, part.at[1]).start()
+    joined = attend(at.share_of(True, False))
+    summed = mm(joined, wp_tight[...])
+    core_copy(0, part.at[0]).wait_recv()
+    y_out[...] = (summed + core_in[0].astype(FLOAT)).astype(HALF)
+    y_copy.start()
+    joined = attend(at.share_of(False, False))
+    summed = mm(joined, wp_tight[...])
+    core_copy(1, part.at[1]).wait_recv()
+    summed = summed + core_in[1].astype(FLOAT)
+    if len(list_i) > 1:
+        gather.forward(list_i[1])
+        push()
+    y_copy.wait_recv()
+    branch[...] = summed + y_in[...].astype(FLOAT) + shared_bias[0:1, :]
+
+    own_rows = rows_at(at.tensor * share, share)
+    chosen = pick(own_rows)
+    middle[...] = x_ref[own_rows, :].astype(FLOAT) + mm(chosen, modk[2]) * branch[...]
+    normed, _ = layer_norm(middle[...])
+    hid_b[own_rows, :] = (normed * (1.0 + mm(chosen, modk[4])) + mm(chosen, modk[3])).astype(HALF)
+
+    def hid_rows(other_y, other_core):
+        return hid_b.at[rows_at(at.share_of(other_y, other_core) * share, share)]
+
+    own_hid = hid_rows(False, False)
+    to_core = remote(own_hid, own_hid, gat_send.at[0], gat_recv.at[0], at.core_peer())
+    to_y = remote(own_hid, own_hid, gat_send.at[1], gat_recv.at[1], at.y_peer())
+    to_y.start()
+    to_core.start()
+    across = hid_rows(True, False)
+    onward = remote(across, across, gat_send.at[2], gat_recv.at[2], at.core_peer())
+    for piece in list_i[2:]:
+        gather.forward(piece)
+        push()
+    remote(across, across, gat_send.at[1], gat_recv.at[1], at.y_peer()).wait_recv()
+    onward.start()
+    for piece in list_i:
+        gather.arrive(piece)
+    beside = hid_rows(False, True)
+    remote(beside, beside, gat_send.at[0], gat_recv.at[0], at.core_peer()).wait_recv()
+    far = hid_rows(True, True)
+    remote(far, far, gat_send.at[2], gat_recv.at[2], at.core_peer()).wait_recv()
+    gather.forward(list_o[0])
+    push()
+
+    def inner_block(index, carry):
+        rows = rows_at(index * share, share)
+        pre = mm(hid_b[rows, :], wi_full[...]) + inner_bias[...]
+        factor = math.sqrt(2.0 / math.pi)
+        squared = pre * pre
+        bend = jnp.tanh(factor * (pre + 0.044715 * squared * pre))
+        act[rows, :] = (0.5 * pre * (1.0 + bend)).astype(HALF)
+        slope[rows, :] = (
+            0.5 * (1.0 + bend)
+            + 0.5 * pre * (1.0 - bend * bend) * (factor * (1.0 + (3 * 0.044715) * squared))
+        ).astype(HALF)
+        return carry
+
+    lax.fori_loop(0, tokens // share, inner_block, 0)
+
+    saves = []
+
+    def save(src, dst):
+        copy = pltpu.make_async_copy(src, dst, save_sem.at[len(saves)])
+        copy.start()
+        saves.append(copy)
+
+    for src, dst in (
+        (wq_full, wq_out), (wp_tight, wp_out), (wi_full, wi_out), (hid_a, hid_a_out), (heads, heads_out),
+        (lse, lse_out), (att, att_out), (hid_b, hid_b_out), (act, act_out), (slope, slope_out),
+        (branch, branch_out), (middle, middle_out), (modk, modk_out),
+    ):
+        save(src, dst)
+    for piece in list_o[1:]:
+        gather.forward(piece)
+        push()
+    for piece in list_o:
+        gather.arrive(piece)
+    save(wo_full, wo_out)
+
+    def outer_block(index, carry):
+        rows = rows_at(index * share, share)
+        ff_part[rows, :] = mm(act[rows, :], wo_full[...]).astype(HALF)
+        return carry
+
+    lax.fori_loop(0, tokens // share, outer_block, 0)
+    save(ff_part, part_out)
+
+    for step in range(1, at.tensor_count):
+        mod_copy(step).wait_send()
+    core_copy(0, part.at[0]).wait_send()
+    core_copy(1, part.at[1]).wait_send()
+    y_copy.wait_send()
+    to_core.wait_send()
+    to_y.wait_send()
+    onward.wait_send()
+    for piece in range(max(0, last - 2), last):
+        gather.sent(piece)
+    for piece in range(last):
+        gather.finish(piece)
+    for copy in saves:
+        copy.wait()
+
+
+def any_spec():
+    return pl.BlockSpec(memory_space=pl.ANY)
+
+
+def vmem_spec():
+    return pl.BlockSpec(memory_space=pltpu.VMEM)
+
+
+def sizes_of(block_input, segment_ids, qkv_weight, inner_weight):
+    dp_count, tensor_count = lax.axis_size("dp"), lax.axis_size("tensor")
+    tokens, width = block_input.shape
+    return {
+        "dp": dp_count,
+        "tensor": tensor_count,
+        "tokens": tokens,
+        "rows": segment_ids.shape[0],
+        "width": width,
+        "columns": qkv_weight.shape[2],
+        "hidden": inner_weight.shape[1],
+        "shard": qkv_weight.shape[0],
+        "share": tokens // tensor_count,
+    }
+
+
+def kernels_fit(sizes):
+    return (
+        sizes["tensor"] == 2 * CORES
+        and sizes["rows"] == 1
+        and sizes["share"] % 128 == 0
+        and sizes["width"] % 128 == 0
+        and sizes["hidden"] % 128 == 0
+        and sizes["shard"] % 16 == 0
+        and sizes["columns"] % 32 == 0
+    )
+
+
+def run_forward(sizes, block_input, segment_ids, cond_act, ada_weight, head_biases, inner_bias,
+                shared_biases, wq, wp, wi, wo):
+    tokens, width, columns, share = (sizes[k] for k in ("tokens", "width", "columns", "share"))
+    hidden, dp_count, tensor_count = sizes["hidden"], sizes["dp"], sizes["tensor"]
+    nheads, segs = columns // HD, cond_act.shape[0]
+    own_rows = columns // dp_count
+    pad_rows = wp.shape[0]
+    xs = line_length(dp_count)
+    zs = dp_count // xs
+    units = sum(w.shape[0] // 48 if w.shape[0] % 48 == 0 else 1 for w in (wq, wp, wi, wo))
+    tight = jnp.arange(columns)
+    place = (tight // own_rows * pad_rows + tight % own_rows)[:, None] == jnp.arange(dp_count * pad_rows)
+    shapes = [
+        ((width, 3 * columns), HALF), ((columns, width), HALF), ((width, hidden), HALF),
+        ((hidden, width), HALF), ((tokens, width), HALF), ((3 * nheads, tokens, HD), HALF),
+        ((nheads, tokens, 1), FLOAT), ((tokens, columns), HALF), ((tokens, width), HALF),
+        ((tokens, hidden), HALF), ((tokens, hidden), HALF), ((tokens, width), HALF),
+        ((share, width), FLOAT), ((share, width), FLOAT), ((6, 2 * segs, width), HALF),
+    ]
+    vmem = pltpu.VMEM
+    dma = pltpu.SemaphoreType.DMA
+    scratch = [
+        vmem((width, 3 * columns), HALF), vmem((dp_count * pad_rows, width), HALF),
+        vmem((columns, width), HALF), vmem((width, hidden), HALF), vmem((hidden, width), HALF),
+        vmem((tokens, width), HALF), vmem((3 * nheads, tokens, HD), HALF),
+        vmem((nheads, tokens, 1), FLOAT), vmem((nheads, share, HD), FLOAT),
+        vmem((tokens, columns), HALF), vmem((2, share, width), HALF), vmem((2, share, width), HALF),
+        vmem((share, width), HALF), vmem((share, width), HALF), vmem((tokens, width), HALF),
+        vmem((tokens, hidden), HALF), vmem((tokens, hidden), HALF), vmem((tokens, width), HALF),
+        vmem((share, width), FLOAT), vmem((share, width), FLOAT), vmem((6, 2 * segs, width), HALF),
+        vmem((tensor_count, 6, segs, columns), FLOAT), vmem((2, columns, width), FLOAT),
+        dma((units, zs - 1)), dma((units, zs - 1)), dma((units, zs, xs - 1)), dma((units, zs, xs - 1)),
+        dma((tensor_count - 1,)), dma((tensor_count - 1,)), dma((3,)), dma((3,)), dma((3,)), dma((3,)),
+        dma((2,)), dma((15,)),
+    ]
+    return pl.pallas_call(
+        functools.partial(forward_kernel, sizes),
+        out_shape=[jax.ShapeDtypeStruct(s, t) for s, t in shapes],
+        in_specs=[vmem_spec()] * 4 + [any_spec()] + [vmem_spec()] * 9,
+        out_specs=[any_spec()] * len(shapes),
+        scratch_shapes=scratch,
+        name="forward",
+        compiler_params=pltpu.CompilerParams(
+            collective_id=1, has_side_effects=True, vmem_limit_bytes=VMEM_BYTES
+        ),
+    )(
+        block_input, segment_ids.reshape(tokens, 1), segment_ids, cond_act, ada_weight,
+        head_biases[3:].reshape(6, 1, columns), head_biases[:3].reshape(1, 3 * columns),
+        inner_bias.reshape(1, hidden), shared_biases, place.astype(HALF), wq, wp, wi, wo,
+    )
+
+
+def on_device_general(
     block_input,
     conditions,
     segment_ids,
@@ -185,7 +713,7 @@
     condition_row_block = jnp.einsum(
         "btu,ua->bta", condition_select, conditions, precision=PRECISION_MAX
     )
-    cond_act, silu_back = jax.vjp(silu, condition_row_block)
+    cond_act = silu(condition_row_block)
     local_mod = (
         jnp.einsum("rsd,kcd->rskc", cond_act, ada_weight, precision=PRECISION_MAX)
         + head_biases[3:][None, None]
@@ -209,16 +737,18 @@
     total_rows = [total_row]
     attended = jnp.stack(attended_rows).reshape(token_count, columns).astype(HALF)
     attn_partial = jnp.dot(attended, proj_full, preferred_element_type=FLOAT)
-    branch_one = lax.psum(attn_partial, "tensor") + shared_biases[0]
-    middle = inputs + token_mod[:, 2] * branch_one
+    share_mod = share(token_mod)
+    branch_one = sum_to_shares(attn_partial) + shared_biases[0]
+    middle = share(inputs) + share_mod[:, 2] * branch_one
     normed_two, inv_two = normalize(middle)
-    hidden_two = (normed_two * (1.0 + token_mod[:, 4]) + token_mod[:, 3]).astype(HALF)
+    hidden_two_share = (normed_two * (1.0 + share_mod[:, 4]) + share_mod[:, 3]).astype(HALF)
+    hidden_two = lax.all_gather(hidden_two_share, "tensor", axis=0, tiled=True)
     pre_act = jnp.dot(hidden_two, inner_full, preferred_element_type=FLOAT) + inner_bias
     act_values, gelu_back = jax.vjp(gelu_tanh, pre_act)
     act_low = act_values.astype(HALF)
     ff_partial = jnp.dot(act_low, outer_full, preferred_element_type=FLOAT)
-    branch_two = lax.psum(ff_partial, "tensor") + shared_biases[1]
-    output = middle + token_mod[:, 5] * branch_two
+    branch_two = sum_to_shares(ff_partial) + shared_biases[1]
+    output = middle + share_mod[:, 5] * branch_two
     grad_out = cotangent.astype(FLOAT)
     grad_two = (grad_out * token_mod[:, 5]).astype(HALF)
     outer_grad = jnp.einsum("nf,nd->fd", act_low, grad_two, preferred_element_type=FLOAT)
@@ -226,11 +756,13 @@
     grad_pre = gelu_back(grad_act)[0].astype(HALF)
     inner_grad = jnp.einsum("nd,nf->df", hidden_two, grad_pre, preferred_element_type=FLOAT)
     back_two_partial = jnp.einsum("nf,df->nd", grad_pre, inner_full, preferred_element_type=FLOAT)
-    grad_hidden_two = lax.psum(back_two_partial, "tensor")
-    grad_middle = grad_out + norm_back(
-        grad_hidden_two * (1.0 + token_mod[:, 4]), normed_two, inv_two
-    )
-    grad_one = (grad_middle * token_mod[:, 2]).astype(HALF)
+    grad_hidden_two = sum_to_shares(back_two_partial)
+    grad_out_share = share(grad_out)
+    grad_middle = grad_out_share + norm_back(
+        grad_hidden_two * (1.0 + share_mod[:, 4]), normed_two, inv_two
+    )
+    grad_one_share = (grad_middle * share_mod[:, 2]).astype(HALF)
+    grad_one = lax.all_gather(grad_one_share, "tensor", axis=0, tiled=True)
     proj_grad = jnp.einsum("nc,nd->cd", attended, grad_one, preferred_element_type=FLOAT)
     grad_attended = jnp.einsum(
         "nd,cd->nc", grad_one, proj_full, preferred_element_type=FLOAT
@@ -243,53 +775,47 @@
     grad_qkv = jnp.stack(grad_qkv_rows).reshape(token_count, 3, columns).astype(HALF)
     qkv_grad = jnp.einsum("nd,nkc->dkc", hidden_one, grad_qkv, preferred_element_type=FLOAT)
     back_one_partial = jnp.einsum("nkc,dkc->nd", grad_qkv, qkv_full, preferred_element_type=FLOAT)
-    grad_hidden_one = lax.psum(back_one_partial, "tensor")
-    grad_input = grad_middle + norm_back(
-        grad_hidden_one * (1.0 + token_mod[:, 1]), normed_one, inv_one
-    )
-    offset = lax.axis_index("tensor") * columns
-
-    def local_columns(values):
-        return lax.dynamic_slice_in_dim(values, offset, columns, 1)
-
-    hidden_one_local = local_columns(grad_hidden_one)
-    hidden_two_local = local_columns(grad_hidden_two)
-    token_contributions = jnp.stack(
+    grad_hidden_one = sum_to_shares(back_one_partial)
+    normed_one_share, inv_one_share = share(normed_one), share(inv_one)
+    input_out = grad_middle + norm_back(
+        grad_hidden_one * (1.0 + share_mod[:, 1]), normed_one_share, inv_one_share
+    )
+    block_out = output.astype(HALF)
+    contributions = jnp.concatenate(
         [
-            hidden_one_local,
-            hidden_one_local * local_columns(normed_one),
-            local_columns(grad_middle) * local_columns(branch_one),
-            hidden_two_local,
-            hidden_two_local * local_columns(normed_two),
-            local_columns(grad_out) * local_columns(branch_two),
+            grad_hidden_one,
+            grad_hidden_one * normed_one_share,
+            grad_middle * branch_one,
+            grad_hidden_two,
+            grad_hidden_two * normed_two,
+            grad_out_share * branch_two,
         ],
         axis=1,
-    ).reshape(rows_local, row_length, 6, columns)
-    grad_mod = jnp.einsum("rls,rlkc->rskc", seg_pick, token_contributions, precision=PRECISION_MAX)
-    block_out = share(output).astype(HALF)
-    input_out = share(grad_input)
-    grad_cond_act = jnp.einsum("rskc,kcd->rsd", grad_mod, ada_weight, precision=PRECISION_MAX)
-    gradient_condition_rows = silu_back(grad_cond_act)[0]
-    condition_portion = jnp.einsum(
-        "tko,tkc->oc", condition_select, gradient_condition_rows, precision=PRECISION_MAX
-    )
-    cond_grad = lax.psum(condition_portion, ("dp", "tensor"))
-    head_bias_grad = jnp.concatenate(
-        [jnp.sum(grad_qkv.astype(FLOAT), axis=0), jnp.sum(grad_mod, axis=(0, 1))], axis=0
-    )
+    )
+    pick_share = share(seg_pick.reshape(token_count, seg_count))
+    cond_pick = jnp.dot(pick_share, condition_select[0], precision=PRECISION_MAX)
+    cond_sums = jnp.einsum("lq,lc->qc", cond_pick, contributions, precision=PRECISION_MAX)
+    cond_sums = cond_sums.reshape(-1, 6, lax.axis_size("tensor"), columns)
+    cond_sums = lax.psum_scatter(cond_sums, "tensor", scatter_dimension=2, tiled=True)[:, :, 0]
+    cond_total = lax.psum(cond_sums, "dp")
+    all_act, all_silu_back = jax.vjp(silu, conditions)
+    grad_all_act = jnp.einsum("qkc,kcd->qd", cond_total, ada_weight, precision=PRECISION_MAX)
+    cond_grad = all_silu_back(lax.psum(grad_all_act, "tensor"))[0]
+    head_bias_grad = jnp.sum(grad_qkv.astype(FLOAT), axis=0)
     inner_bias_grad = jnp.sum(grad_pre.astype(FLOAT), axis=0)
     shared_bias_grad = jnp.stack(
         [jnp.sum(grad_one.astype(FLOAT), axis=0), jnp.sum(grad_two.astype(FLOAT), axis=0)]
     )
-    ada_grad = jnp.einsum("rsd,rskc->kcd", cond_act, grad_mod, precision=PRECISION_MAX)
-    ada_total, head_total, inner_bias_total, shared_total = lax.psum(
-        (ada_grad, head_bias_grad, inner_bias_grad, shared_bias_grad), "dp"
-    )
+    ada_total = jnp.einsum("qd,qkc->kcd", all_act, cond_total, precision=PRECISION_MAX)
+    head_total, inner_bias_total, shared_total = lax.psum(
+        (head_bias_grad, inner_bias_grad, shared_bias_grad), "dp"
+    )
+    head_total = jnp.concatenate([head_total, jnp.sum(cond_total, axis=0)], axis=0)
     qkv_shard, proj_shard, inner_shard, outer_shard = (
-        lax.psum_scatter(qkv_grad, "dp", scatter_dimension=0, tiled=True),
-        lax.psum_scatter(proj_grad, "dp", scatter_dimension=0, tiled=True),
-        lax.psum_scatter(inner_grad, "dp", scatter_dimension=0, tiled=True),
-        lax.psum_scatter(outer_grad, "dp", scatter_dimension=0, tiled=True),
+        sum_to_owners(qkv_grad),
+        sum_to_owners(proj_grad),
+        sum_to_owners(inner_grad),
+        sum_to_owners(outer_grad),
     )
     qkv_new = adam_update(qkv_weight, qkv_shard, qkv_first, qkv_second, RATES[0])
     proj_new = adam_update(proj_weight, proj_shard, proj_first, proj_second, RATES[1])
@@ -338,6 +864,200 @@
     )
 
 
+def on_device_kernels(
+    block_input,
+    conditions,
+    segment_ids,
+    segment_cond,
+    cotangent,
+    qkv_weight,
+    proj_weight,
+    inner_weight,
+    outer_weight,
+    ada_weight,
+    head_biases,
+    inner_bias,
+    shared_biases,
+    qkv_first,
+    proj_first,
+    inner_first,
+    outer_first,
+    ada_first,
+    head_biases_first,
+    inner_bias_first,
+    shared_biases_first,
+    qkv_second,
+    proj_second,
+    inner_second,
+    outer_second,
+    ada_second,
+    head_biases_second,
+    inner_bias_second,
+    shared_biases_second,
+):
+    columns = qkv_weight.shape[2]
+    heads_local = columns // HD
+    rows_local = segment_ids.shape[0]
+    row_length = segment_ids.shape[1]
+    token_count = rows_local * row_length
+    seg_count = segment_cond.shape[1]
+    width = block_input.shape[1]
+    share_count = token_count // lax.axis_size("tensor")
+    share_start = lax.axis_index("tensor") * share_count
+
+    def share(values):
+        return lax.dynamic_slice_in_dim(values, share_start, share_count, 0)
+
+    condition_select = (
+        segment_cond[:, :, None] == jnp.arange(conditions.shape[0])[None, None, :]
+    ).astype(FLOAT)
+    condition_row_block = jnp.einsum(
+        "btu,ua->bta", condition_select, conditions, precision=PRECISION_MAX
+    )
+    cond_act = silu(condition_row_block)
+    sizes = sizes_of(block_input, segment_ids, qkv_weight, inner_weight)
+    grow = -proj_weight.shape[0] % 16
+    (qkv_full, proj_full, inner_full, outer_full, hidden_one, heads, log_sums, attended, hidden_two,
+     act_low, slope, ff_partial, branch_one, middle, modk) = run_forward(
+        sizes, block_input, segment_ids, cond_act[0], ada_weight, head_biases, inner_bias, shared_biases,
+        qkv_weight.astype(HALF).reshape(-1, 3 * columns),
+        jnp.pad(proj_weight.astype(HALF), ((0, grow), (0, 0))),
+        inner_weight.astype(HALF), outer_weight.astype(HALF),
+    )
+    qkv_full = qkv_full.reshape(width, 3, columns)
+    full_mod = (modk[:, :seg_count].astype(FLOAT) + modk[:, seg_count:].astype(FLOAT)).transpose(1, 0, 2)[None]
+    seg_pick = (segment_ids[:, :, None] == jnp.arange(seg_count)[None, None, :]).astype(FLOAT)
+    token_mod = jnp.einsum("rls,rskd->rlkd", seg_pick, full_mod, precision=PRECISION_MAX).reshape(
+        token_count, 6, width
+    )
+    share_mod = share(token_mod)
+    row_qkv = heads.reshape(1, 3, heads_local, token_count, HD).transpose(0, 3, 1, 2, 4)
+    total_rows = [log_sums.reshape(heads_local, 2, token_count // 2).transpose(1, 0, 2)]
+    inputs = block_input.astype(FLOAT)
+    normed_one, inv_one = normalize(inputs)
+    normed_two, inv_two = normalize(middle)
+    branch_two = sum_to_shares(ff_partial) + shared_biases[1]
+    output = middle + share_mod[:, 5] * branch_two
+    grad_out = cotangent.astype(FLOAT)
+    grad_two = (grad_out * token_mod[:, 5]).astype(HALF)
+    outer_grad = jnp.einsum("nf,nd->fd", act_low, grad_two, preferred_element_type=FLOAT)
+    grad_act = jnp.einsum("nd,fd->nf", grad_two, outer_full, preferred_element_type=FLOAT)
+    grad_pre = (grad_act * slope.astype(FLOAT)).astype(HALF)
+    inner_grad = jnp.einsum("nd,nf->df", hidden_two, grad_pre, preferred_element_type=FLOAT)
+    back_two_partial = jnp.einsum("nf,df->nd", grad_pre, inner_full, preferred_element_type=FLOAT)
+    grad_hidden_two = sum_to_shares(back_two_partial)
+    grad_out_share = share(grad_out)
+    grad_middle = grad_out_share + norm_back(
+        grad_hidden_two * (1.0 + share_mod[:, 4]), normed_two, inv_two
+    )
+    grad_one_share = (grad_middle * share_mod[:, 2]).astype(HALF)
+    grad_one = lax.all_gather(grad_one_share, "tensor", axis=0, tiled=True)
+    proj_grad = jnp.einsum("nc,nd->cd", attended, grad_one, preferred_element_type=FLOAT)
+    grad_attended = jnp.einsum(
+        "nd,cd->nc", grad_one, proj_full, preferred_element_type=FLOAT
+    ).astype(HALF)
+    grad_rows = grad_attended.reshape(rows_local, row_length, heads_local, HD)
+    row = 0
+    grad_qkv_rows = [
+        attend_backward(row_qkv[row], segment_ids[row], grad_rows[row], total_rows[row])
+    ]
+    grad_qkv = jnp.stack(grad_qkv_rows).reshape(token_count, 3, columns).astype(HALF)
+    qkv_grad = jnp.einsum("nd,nkc->dkc", hidden_one, grad_qkv, preferred_element_type=FLOAT)
+    back_one_partial = jnp.einsum("nkc,dkc->nd", grad_qkv, qkv_full, preferred_element_type=FLOAT)
+    grad_hidden_one = sum_to_shares(back_one_partial)
+    normed_one_share, inv_one_share = share(normed_one), share(inv_one)
+    input_out = grad_middle + norm_back(
+        grad_hidden_one * (1.0 + share_mod[:, 1]), normed_one_share, inv_one_share
+    )
+    block_out = output.astype(HALF)
+    contributions = jnp.concatenate(
+        [
+            grad_hidden_one,
+            grad_hidden_one * normed_one_share,
+            grad_middle * branch_one,
+            grad_hidden_two,
+            grad_hidden_two * normed_two,
+            grad_out_share * branch_two,
+        ],
+        axis=1,
+    )
+    pick_share = share(seg_pick.reshape(token_count, seg_count))
+    cond_pick = jnp.dot(pick_share, condition_select[0], precision=PRECISION_MAX)
+    cond_sums = jnp.einsum("lq,lc->qc", cond_pick, contributions, precision=PRECISION_MAX)
+    cond_sums = cond_sums.reshape(-1, 6, lax.axis_size("tensor"), columns)
+    cond_sums = lax.psum_scatter(cond_sums, "tensor", scatter_dimension=2, tiled=True)[:, :, 0]
+    cond_total = lax.psum(cond_sums, "dp")
+    all_act, all_silu_back = jax.vjp(silu, conditions)
+    grad_all_act = jnp.einsum("qkc,kcd->qd", cond_total, ada_weight, precision=PRECISION_MAX)
+    cond_grad = all_silu_back(lax.psum(grad_all_act, "tensor"))[0]
+    head_bias_grad = jnp.sum(grad_qkv.astype(FLOAT), axis=0)
+    inner_bias_grad = jnp.sum(grad_pre.astype(FLOAT), axis=0)
+    shared_bias_grad = jnp.stack(
+        [jnp.sum(grad_one.astype(FLOAT), axis=0), jnp.sum(grad_two.astype(FLOAT), axis=0)]
+    )
+    ada_total = jnp.einsum("qd,qkc->kcd", all_act, cond_total, precision=PRECISION_MAX)
+    head_total, inner_bias_total, shared_total = lax.psum(
+        (head_bias_grad, inner_bias_grad, shared_bias_grad), "dp"
+    )
+    head_total = jnp.concatenate([head_total, jnp.sum(cond_total, axis=0)], axis=0)
+    qkv_shard, proj_shard, inner_shard, outer_shard = (
+        sum_to_owners(qkv_grad),
+        sum_to_owners(proj_grad),
+        sum_to_owners(inner_grad),
+        sum_to_owners(outer_grad),
+    )
+    qkv_new = adam_update(qkv_weight, qkv_shard, qkv_first, qkv_second, RATES[0])
+    proj_new = adam_update(proj_weight, proj_shard, proj_first, proj_second, RATES[1])
+    inner_new = adam_update(inner_weight, inner_shard, inner_first, inner_second, RATES[2])
+    outer_new = adam_update(outer_weight, outer_shard, outer_first, outer_second, RATES[3])
+    ada_new = adam_update(ada_weight, ada_total, ada_first, ada_second, RATES[4])
+    head_new = adam_update(head_biases, head_total, head_biases_first, head_biases_second, RATES[5])
+    inner_bias_new = adam_update(
+        inner_bias, inner_bias_total, inner_bias_first, inner_bias_second, RATES[6]
+    )
+    shared_new = adam_update(
+        shared_biases, shared_total, shared_biases_first, shared_biases_second, RATES[7]
+    )
+    return (
+        block_out,
+        input_out,
+        cond_grad,
+        qkv_new[0],
+        proj_new[0],
+        inner_new[0],
+        outer_new[0],
+        ada_new[0],
+        head_new[0],
+        inner_bias_new[0],
+        shared_new[0],
+        qkv_new[1],
+        proj_new[1],
+        inner_new[1],
+        outer_new[1],
+        ada_new[1],
+        head_new[1],
+        inner_bias_new[1],
+        shared_new[1],
+        qkv_new[2],
+        proj_new[2],
+        inner_new[2],
+        outer_new[2],
+        ada_new[2],
+        head_new[2],
+        inner_bias_new[2],
+        shared_new[2],
+        qkv_new[0].astype(HALF),
+        proj_new[0].astype(HALF),
+        inner_new[0].astype(HALF),
+        outer_new[0].astype(HALF),
+    )
+
+
+def on_device(*args):
+    sizes = sizes_of(args[0], args[2], args[5], args[7])
+    return (on_device_kernels if kernels_fit(sizes) else on_device_general)(*args)
+
+
 def solution(mesh):
     in_specs = (
         P("dp", None),

time: 1480 us -> 725 us (0.49)
  waiting for transfers between devices: 949 us -> 307 us
  Pallas kernels: 0 us -> 121 us
  blocking collectives: 167 us -> 61 us
  other arithmetic: 131 us -> 53.3 us
  matrix products: 153 us -> 109 us
    psum x5 -> x2, waiting for transfers between devices: 690 us -> 78.8 us  [the longest x1 70.7 us: on_device_kernels(): cond_total = lax.psum(cond_sums, 'dp')]
    pallas_call x0 -> x1, Pallas kernels: none -> 121 us  [run_forward(): pl.pallas_call(functools.partial(forward_kernel, sizes), out_shape=[jax.S...]
    all_gather x3 -> x1, waiting for transfers between devices: 82.5 us -> 4.42 us  [on_device_kernels(): grad_one = lax.all_gather(grad_one_share, 'tensor', axis=0, tiled=True)]
    all_gather x2 -> x0, blocking collectives: 67.5 us -> none  [the longest x1 35.4 us: on_device(): lax.all_gather(proj_weight.astype(HALF), 'dp', axis=0, tiled=True)]
    reduce_scatter x3 -> x7, waiting for transfers between devices: 173 us -> 223 us  [the longest x3 148 us: sum_to_owners(): lax.psum_scatter(partial.astype(HALF), 'dp', scatter_dimension=0, tiled=T...]
    dot_general x21 -> x14, matrix products: 122 us -> 87.7 us  [the longest x1 21.2 us: on_device_kernels(): jnp.einsum('qd,qkc->kcd', all_act, cond_total, precision=PRECISION_MAX)]
    reduce_sum x5 -> x4, other arithmetic: 33.8 us -> 4.51 us  [the longest x1 3.75 us: on_device_kernels(): jnp.sum(grad_two.astype(FLOAT), axis=0)]
    unnamed x1, blocking collectives: 53.9 us -> 26.9 us
  transfers between devices with their start and end apart: 13 -> 12, of which waited for: 10 -> 9; matrix products, arithmetic and copies ran while one was open for 16% -> 17% of each run, Pallas kernels for 0% -> 0%
where the time goes in v1:
time: 725 us; the launch traced here: 721 us
  waiting for transfers between devices  307 us (42%)
  Pallas kernels  121 us (17%)
  matrix products  109 us (15%)
  blocking collectives  61 us (8%)
  other arithmetic  53.3 us (7%)
  local copies, waits for them, and re-layouts  46.1 us (6%)
  between operations  15.9 us (2%)
    reduce_scatter x3, waiting for transfers between devices, sum_to_owners(): lax.psum_scatter(partial.astype(HALF), 'dp', scatter_dimension=0, tiled=T...  148 us
    pallas_call x1, Pallas kernels, run_forward(): pl.pallas_call(functools.partial(forward_kernel, sizes), out_shape=[jax.S...  121 us
    reduce_scatter x3, waiting for transfers between devices, sum_to_shares(): lax.psum_scatter(partial.astype(HALF), 'tensor', scatter_dimension=0, til...  74.9 us
    psum x1, waiting for transfers between devices, on_device_kernels(): cond_total = lax.psum(cond_sums, 'dp')  70.7 us
    psum x1, blocking collectives, on_device_kernels(): lax.psum((head_bias_grad, inner_bias_grad, shared_bias_grad), 'dp')  34.1 us
    unnamed x1, blocking collectives  26.9 us
    dot_general x1, matrix products, on_device_kernels(): jnp.einsum('qd,qkc->kcd', all_act, cond_total, precision=PRECISION_MAX)  21.2 us
    dot_general x1, matrix products, on_device_kernels(): jnp.einsum('rls,rskd->rlkd', seg_pick, full_mod, precision=PRECISION_MAX)  16.1 us
  transfers between devices with their start and end apart: 12, of which 9 were waited for; matrix products, arithmetic and copies ran while one was open for 17% of the time, Pallas kernels for 0%

profile of v1, /device:TPU:0, one launch (start us, length us, event | category | flops | bytes accessed | tf_op | source)
XLA Modules:
  0.0 721.0 jit_solution(13184987121413149512)
XLA Ops:
  19.5 121.1 %forward.1 = (bf16[1152,864]{1,0:T(8,128)(2,1)}, bf16[288,1152]{1,0:T(8,128)(2,1)}, bf16[1152,1152]{1,0:T(8,128)(2,1)}, bf16[1152,1152]{1,0:T(8,128)(2,1)}, bf16...) custom-call(bf16[1024,1152]{1,0:T(8,128)(2,1)} %x_ref.1, ...), custom_call_target="tpu_custom_call" | custom-call | tf_op jit(solution)/shard_map/forward/pallas_call | solution.py:643
  140.6 16.1 %fusion.52 = f32[1024,6,1152]{2,0,1:T(8,128)} fusion(bf16[6,16,1152]{2,1,0:T(8,128)(2,1)} %get-tuple-element.106, s32[1024]{0:T(1024)S(1)} %bitcast.191), kind=kOutput, calls=%fused_computation.110 | convolution fusion | flops 679651328 | bytes 28536832 | tf_op jit(solution)/shard_map/rls,rskd->rlkd/dot_general | solution.py:930
  160.6 4.4 convert_reduce_fusion.3
  166.4 4.8 convolution_convert_fusion.3
  175.7 29.9 %reduce-scatter.12.cloned.1.call-done = bf16[256,1152]{1,0:T(8,128)(2,1)} async-done(((bf16[1024,1152]{1,0:T(8,128)(2,1)}), bf16[256,1152]{1,0:T(8,128)(2,1)}) %reduce-scatter.12.cloned.1.call-update) | async-done | bytes 589840 | tf_op jit(solution)/shard_map/reduce_scatter | solution.py:136
  207.5 33.9 %reduce-scatter.10.cloned.1.call-done = bf16[256,1152]{1,0:T(8,128)(2,1)} async-done(((bf16[1024,1152]{1,0:T(8,128)(2,1)}), bf16[256,1152]{1,0:T(8,128)(2,1)}) %reduce-scatter.10.cloned.1.call-update) | async-done | bytes 589840 | tf_op jit(solution)/shard_map/reduce_scatter | solution.py:136
  241.4 4.6 fusion.40
  250.2 4.4 copy.80
  265.9 4.4 all-gather.2.cloned.1.call-done
  278.6 29.2 %while.15 = (s32[]{:T(128)}, f32[1024,4,72]{0,2,1:T(8,128)S(1)}, f32[1024,4,72]{0,2,1:T(8,128)}, bf16[2,512,4,72]{1,3,2,0:T(8,128)(2,1)}, bf16[2,512,4,72]{1,3,2...) while((s32[]{:T(128)}, f32[1024,4,72]{0,2,1:T(8,128)S(1)}, ...), condition=%wide.region_10.11_spmd.clone, body=%wide.region_8.10_spmd.clone.sunk | while | flops 1543550976 | bytes 92227928 | solution.py:113
  312.7 4.3 bitcast_convert_fusion
  318.6 6.5 convolution_convert_fusion
  326.9 6.4 convolution_convert_fusion.1
  339.0 11.2 %reduce-scatter.14.cloned.1.call-done = bf16[256,1152]{1,0:T(8,128)(2,1)} async-done(((bf16[1024,1152]{1,0:T(8,128)(2,1)}), bf16[256,1152]{1,0:T(8,128)(2,1)}) %reduce-scatter.14.cloned.1.call-update) | async-done | bytes 589840 | tf_op jit(solution)/shard_map/reduce_scatter | solution.py:136
  365.5 7.1 convolution_convert_fusion.2
  374.6 50.2 %reduce-scatter.22.cloned.1.call-done = bf16[144,1152]{1,0:T(8,128)(2,1)} async-done(((bf16[1152,1152]{1,0:T(8,128)(2,1)}), bf16[144,1152]{1,0:T(8,128)(2,1)}) %reduce-scatter.22.cloned.1.call-update) | async-done | bytes 331792 | tf_op jit(solution)/shard_map/reduce_scatter | solution.py:142
  427.7 70.8 %reduce-scatter.20.cloned.1.call-done = bf16[144,1152]{1,0:T(8,128)(2,1)} async-done(((bf16[1152,1152]{1,0:T(8,128)(2,1)}), bf16[144,1152]{1,0:T(8,128)(2,1)}) %reduce-scatter.20.cloned.1.call-update) | async-done | bytes 331792 | tf_op jit(solution)/shard_map/reduce_scatter | solution.py:142
  502.9 26.9 %fusion = bf16[48,1152]{1,0:T(8,128)(2,1)S(1)} fusion(bf16[288,1152]{1,0:T(8,128)(2,1)S(1)} %convolution_convert_fusion.4), kind=kCustom, calls=%all-reduce-scatter | all-reduce-scatter fusion | flops 442369 | bytes 774656
  536.8 34.1 %all-reduce.3 = (f32[3,288]{1,0:T(4,128)S(1)}, f32[1152]{0:T(1024)S(1)}, f32[2,1152]{1,0:T(2,128)S(1)}) all-reduce(f32[3,288]{1,0:T(4,128)S(1)} %convert_reduce_fusion.4, f32[1152]{0:T(1024)S(1)} %copy-done.59, f32[2,1152]{1,0:T(2,128)S(1)} %pad_maximum_fusion.2), channel_id=1, replica_groups=mesh['dp'=8,'tensor'=4] {'dp'}, use_global_device_ids=true, to_apply=%region_22.23 | all-reduce | flops 4320 | bytes 34560 | tf_op jit(solution)/shard_map/psum | solution.py:999
  573.9 27.3 %reduce-scatter.18.cloned.1.call-done = bf16[144,3,288]{2,0,1:T(8,128)(2,1)} async-done(((bf16[1152,3,288]{2,0,1:T(8,128)(2,1)}), bf16[144,3,288]{2,0,1:T(8,128)(2,1)}) %reduce-scatter.18.cloned.1.call-update) | async-done | bytes 248848 | tf_op jit(solution)/shard_map/reduce_scatter | solution.py:142
  604.3 70.7 %all-reduce.7.cloned.1.call-done = f32[32,6,288]{2,0,1:T(8,128)} async-done(((f32[32,6,288]{2,0,1:T(8,128)}), f32[32,6,288]{2,0,1:T(8,128)}) %all-reduce.7.cloned.1.call-update) | async-done | bytes 221200 | tf_op jit(solution)/shard_map/psum | solution.py:989
  675.0 7.2 convolution_bitcast_fusion
  682.3 21.2 %multiply_subtract_fusion = (f32[6,288,1152]{2,1,0:T(8,128)}, f32[6,288,1152]{2,1,0:T(8,128)}, f32[6,288,1152]{2,1,0:T(8,128)}) fusion(f32[6,288,1152]{2,1,0:T(8,128)} %ada_ref.1, f32[6,288,1152]{2,1,0:T(8,128)} %param.48, f32[6,288,1152]{2,1,0:T(8,128)} %param.56, f32[32,6,288]{2,0,1:T(8,128)S(1)} %copy-done.28, f32[32,1152]{1,0:T(8,128)S(1)} %copy-done.39), kind=kOutput, calls=%fused_computation.36 | convolution fusion | flops 792391680 | bytes 48144384 | tf_op jit(solution)/shard_map/qd,qkc->kcd/dot_general | solution.py:998
  704.2 8.0 %all-reduce.9.cloned.1.call-done = f32[32,1152]{1,0:T(8,128)} async-done(((f32[32,1152]{1,0:T(8,128)}), f32[32,1152]{1,0:T(8,128)}) %all-reduce.9.cloned.1.call-update) | async-done | bytes 147472 | tf_op jit(solution)/shard_map/psum | solution.py:992
  (273 shorter events, 128.9 us)
Async XLA Ops:
  7.2 198.4 %reduce-scatter.12.cloned.1.call-start = ((), (), s32[]{:S(2)}) async-start(), calls=%async_computation.8 | async-start | bytes 2949120 | tf_op jit(solution)/shard_map/reduce_scatter | solution.py:136
  171.3 70.2 %reduce-scatter.10.cloned.1.call-start = ((), (), s32[]{:S(2)}) async-start(), calls=%async_computation.7 | async-start | bytes 2949120 | tf_op jit(solution)/shard_map/reduce_scatter | solution.py:136
  172.0 98.3 %all-gather.2.cloned.1.call-start = ((), (), s32[]{:S(2)}) async-start(), calls=%async_computation.9 | async-start | bytes 2949120 | tf_op jit(solution)/shard_map/all_gather | solution.py:954
  175.4 70.6 %copy-start.49 = (f32[256]{0:T(256)}, f32[256]{0:T(256)S(1)}, u32[]{:S(2)}) copy-start(f32[256]{0:T(256)S(1)} %broadcast_multiply_fusion.9) | copy-start | bytes 3076
  175.7 70.3 %copy-start.53 = (f32[256]{0:T(256)}, f32[256]{0:T(256)S(1)}, u32[]{:S(2)}) copy-start(f32[256]{0:T(256)S(1)} %add_rsqrt_fusion.1) | copy-start | bytes 3076
  246.1 104.1 %reduce-scatter.14.cloned.1.call-start = ((), (), s32[]{:S(2)}) async-start(), calls=%async_computation.10 | async-start | bytes 2949120 | tf_op jit(solution)/shard_map/reduce_scatter | solution.py:136
  317.0 107.7 %reduce-scatter.22.cloned.1.call-start = ((), (), s32[]{:S(2)}) async-start(), calls=%async_computation.16 | async-start | bytes 2985984 | tf_op jit(solution)/shard_map/reduce_scatter | solution.py:142
  325.1 173.3 %reduce-scatter.20.cloned.1.call-start = ((), (), s32[]{:S(2)}) async-start(), calls=%async_computation.15 | async-start | bytes 2985984 | tf_op jit(solution)/shard_map/reduce_scatter | solution.py:142
  333.4 240.5 %reduce-scatter.16.cloned.1.call-start = ((), (), s32[]{:S(2)}) async-start(), calls=%async_computation.11 | async-start | bytes 1474560 | tf_op jit(solution)/shard_map/reduce_scatter | solution.py:988
  365.4 235.9 %reduce-scatter.18.cloned.1.call-start = ((), (), s32[]{:S(2)}) async-start(), calls=%async_computation.14 | async-start | bytes 2985984 | tf_op jit(solution)/shard_map/reduce_scatter | solution.py:142
  372.6 52.1 %copy-start.10 = (f32[144,1152]{1,0:T(8,128)S(1)}, f32[144,1152]{1,0:T(8,128)}, u32[]{:S(2)}) copy-start(f32[144,1152]{1,0:T(8,128)} %param.39) | copy-start | bytes 1990660
  372.6 52.1 %copy-start.34 = (f32[144,1152]{1,0:T(8,128)S(1)}, f32[144,1152]{1,0:T(8,128)}, u32[]{:S(2)}) copy-start(f32[144,1152]{1,0:T(8,128)} %param.47) | copy-start | bytes 1990660
  372.6 52.1 %copy-start.35 = (f32[144,1152]{1,0:T(8,128)S(1)}, f32[144,1152]{1,0:T(8,128)}, u32[]{:S(2)}) copy-start(f32[144,1152]{1,0:T(8,128)} %param.55) | copy-start | bytes 1990660
  372.7 125.8 %copy-start.12 = (f32[144,1152]{1,0:T(8,128)S(1)}, f32[144,1152]{1,0:T(8,128)}, u32[]{:S(2)}) copy-start(f32[144,1152]{1,0:T(8,128)} %param.38) | copy-start | bytes 1990660
  372.7 302.3 %all-reduce.7.cloned.1.call-start = ((), (), s32[]{:S(2)}) async-start(), calls=%async_computation.12 | async-start | bytes 589824 | tf_op jit(solution)/shard_map/psum | solution.py:989
  427.7 74.2 %copy-start.7 = (bf16[1024,1152]{1,0:T(8,128)(2,1)S(1)}, bf16[1024,1152]{1,0:T(8,128)(2,1)}, u32[]{:S(2)}) copy-start(bf16[1024,1152]{1,0:T(8,128)(2,1)} %all-gather.2.cloned.1.call-done) | copy-start | bytes 7077892
  530.0 42.9 %copy-start.33 = (f32[36,1152]{1,0:T(8,128)S(1)}, f32[36,1152]{1,0:T(8,128)}, u32[]{:S(2)}) copy-start(f32[36,1152]{1,0:T(8,128)} %param.37) | copy-start | bytes 497668
  530.0 42.2 %collective-permute-start = (bf16[48,1152]{1,0:T(8,128)(2,1)S(1)}, bf16[48,1152]{1,0:T(8,128)(2,1)S(1)}, u32[]{:S(2)}, u32[]{:S(2)}) collective-permute-start(bf16[48,1152]{1,0:T(8,128)(2,1)S(1)} %fusion), channel_id=1, source_target_pairs={{0,4},{4,8},{8,12},{12,16},{16,20},{20,24},{24,28},{1,5},{5,9},{9,... | collective-permute-start | bytes 331784
  533.5 67.8 %copy-start.13 = (f32[144,3,288]{2,0,1:T(8,128)S(1)}, f32[144,3,288]{2,0,1:T(8,128)}, u32[]{:S(2)}) copy-start(f32[144,3,288]{2,0,1:T(8,128)} %param.36) | copy-start | bytes 1492996
  533.5 67.8 %copy-start.36 = (f32[144,3,288]{2,0,1:T(8,128)S(1)}, f32[144,3,288]{2,0,1:T(8,128)}, u32[]{:S(2)}) copy-start(f32[144,3,288]{2,0,1:T(8,128)} %param.44) | copy-start | bytes 1492996
  533.5 67.7 %copy-start.37 = (f32[144,3,288]{2,0,1:T(8,128)S(1)}, f32[144,3,288]{2,0,1:T(8,128)}, u32[]{:S(2)}) copy-start(f32[144,3,288]{2,0,1:T(8,128)} %param.52) | copy-start | bytes 1492996
  533.6 38.7 %collective-permute-start.1 = (bf16[36,1152]{1,0:T(8,128)(2,1)S(1)}, bf16[36,1152]{1,0:T(8,128)(2,1)S(1)}, u32[]{:S(2)}, u32[]{:S(2)}) collective-permute-start(bf16[36,1152]{1,0:T(8,128)(2,1)S(1)} %slice.56), channel_id=1, source_target_pairs={{0,8},{4,12},{8,16},{12,20},{16,24},{20,28},{1,9},{5,13},{9,17},{1... | collective-permute-start | bytes 248840
  573.9 138.3 %all-reduce.9.cloned.1.call-start = ((), (), s32[]{:S(2)}) async-start(), calls=%async_computation.13 | async-start | bytes 294912 | tf_op jit(solution)/shard_map/psum | solution.py:992
  604.3 78.0 %copy-start.39 = (f32[32,1152]{1,0:T(8,128)S(1)}, f32[32,1152]{1,0:T(8,128)}, u32[]{:S(2)}) copy-start(f32[32,1152]{1,0:T(8,128)} %param.32) | copy-start | bytes 442372
  (62 other events, 617.9 us)
Sparse Core Ops, SparseCore 0:
  171.4 34.2 reduce-scatter.11
  208.3 33.0 reduce-scatter.9
  246.2 24.0 all-gather.1
  317.1 33.0 reduce-scatter.13
  354.1 70.5 reduce-scatter.21
  428.8 69.6 reduce-scatter.19
  501.8 24.7 reduce-scatter.15
  530.8 70.4 reduce-scatter.17
  605.0 70.0 all-reduce.6
  682.4 29.8 all-reduce.8
